TPU v7x, 32 devices: a whole 2x2x4 slice. The times are simulated.
32 devices in a mesh: dp: 16 (over z, y, core), seq: 2 (over x).
Axes of the slice: x: 2, y: 2, z: 4, core: 2. Of those that a mesh axis runs over, the one named last changes fastest.
Arguments:
- tokens: bfloat16 [32, 640, 768], P('dp', 'seq'), may hold values from -6 to 6
- seg_count: int32 [32], P('dp'), may hold values from 5 to 128, as said below
- seg_align: int32 [32, 512], P('dp'), may hold values from 0 to 127, as said below
- cotangent: bfloat16 [32, 640, 768], P('dp', 'seq'), may hold values from -6 to 6
- qkv_weight: bfloat16 [768, 2304], replicated, may hold values from -0.21875 to 0.21875
- query_bias: float32 [768], replicated, may hold values from -3 to 3
- value_bias: float32 [768], replicated, may hold values from -3 to 3
- output_weight: bfloat16 [768, 768], replicated, may hold values from -2 to 2
- output_bias: float32 [768], replicated, may hold values from -3 to 3
- first_gain: float32 [768], replicated, may hold values from 0.1 to 1.9
- first_shift: float32 [768], replicated, may hold values from -3 to 3
- inner_weight: bfloat16 [768, 3072], replicated, may hold values from -0.21875 to 0.21875
- inner_bias: float32 [3072], replicated, may hold values from -3 to 3
- outer_weight: bfloat16 [3072, 768], replicated, may hold values from -0.109375 to 0.109375
- outer_bias: float32 [768], replicated, may hold values from -3 to 3
- second_gain: float32 [768], replicated, may hold values from 0.1 to 1.9
- second_shift: float32 [768], replicated, may hold values from -3 to 3
Outputs:
- block_output: bfloat16 [32, 640, 768], P('dp', 'seq')
- tokens_grad: bfloat16 [32, 640, 768], P('dp', 'seq')
- qkv_weight_grad: float32 [768, 2304], P('dp')
- query_bias_grad: float32 [768], P('dp')
- value_bias_grad: float32 [768], P('dp')
- output_weight_grad: float32 [768, 768], P('dp')
- output_bias_grad: float32 [768], P('dp')
- first_gain_grad: float32 [768], P('dp')
- first_shift_grad: float32 [768], P('dp')
- inner_weight_grad: float32 [768, 3072], P('dp')
- inner_bias_grad: float32 [3072], P('dp')
- outer_weight_grad: float32 [3072, 768], P('dp')
- outer_bias_grad: float32 [768], P('dp')
- second_gain_grad: float32 [768], P('dp')
- second_shift_grad: float32 [768], P('dp')
Inputs may be any that keep to these rules, and one draw needn't show every extreme that they name: `seg_count`: heavy tailed; some document has exactly 128 segment tokens. `seg_align`: below the document's seg_count.
All inputs are finite; a program needn't handle non-finite values.
Results may differ from a plain program's by a relative error of at most 0.015.
Values may be sent and summed in bfloat16 or wider, within the bound.
A program may use at most 192 MiB of HBM per device.

v0:
```python
import jax
import jax.numpy as jnp
from jax import lax
from jax.sharding import PartitionSpec as P

H = 12


LAYOUT_REWARD = 2.0
BLOCKED_SCORE = -1000000000.0
NORM_EPS = 1e-05


def slot_groups(seg_count, seg_align, all_slots):
    doc_count, text_slots = seg_align.shape
    slot_index = jnp.arange(all_slots, dtype=jnp.int32)
    filler = jnp.zeros((doc_count, all_slots - text_slots), jnp.int32)
    padded = jnp.concatenate([seg_align, filler], axis=1)
    is_text = slot_index < text_slots
    groups = jnp.where(is_text[None, :], padded, (slot_index - text_slots)[None, :])
    present_keys = slot_index[None, :] < text_slots + seg_count[:, None]
    return (groups, is_text, present_keys)


def layer_norm(hidden, gain, shift):
    centre = hidden - jnp.mean(hidden, axis=-1, keepdims=True)
    spread = jnp.mean(centre * centre, axis=-1, keepdims=True)
    return centre * lax.rsqrt(spread + NORM_EPS) * gain + shift


def smooth_gate(inner):
    return jax.nn.gelu(inner, approximate=False)


def softmax_rows(logit_scores):
    return jax.nn.softmax(logit_scores, axis=-1)


def project(tokens, qkv_weight, query_bias, value_bias):
    doc_count, slot_count, features = tokens.shape
    token_rows = tokens.reshape(doc_count * slot_count, features)
    pre = jnp.dot(token_rows, qkv_weight, preferred_element_type=jnp.float32)
    queries = (pre[:, :features] + query_bias).astype(jnp.bfloat16)
    own_keys = (
        pre[:, features : 2 * features]
        .astype(jnp.bfloat16)
        .reshape(doc_count, slot_count, features)
    )
    own_values = (
        (pre[:, 2 * features :] + value_bias)
        .astype(jnp.bfloat16)
        .reshape(doc_count, slot_count, features)
    )
    all_keys, values = (
        lax.all_gather(own_keys, "seq", axis=1, tiled=True),
        lax.all_gather(own_values, "seq", axis=1, tiled=True),
    )
    return (queries, all_keys, values)


def local(
    tokens,
    seg_count,
    seg_align,
    cotangent,
    qkv_weight,
    query_bias,
    value_bias,
    output_weight,
    output_bias,
    first_gain,
    first_shift,
    inner_weight,
    inner_bias,
    outer_weight,
    outer_bias,
    second_gain,
    second_shift,
):
    doc_count, slot_count, features = tokens.shape
    row_count = doc_count * slot_count
    head_dim = features // H
    scaling = head_dim ** (-0.5)
    all_slots = slot_count * lax.axis_size("seq")
    row_start = lax.axis_index("seq") * slot_count
    groups, is_text, present_keys = slot_groups(seg_count, seg_align, all_slots)
    group_rows = lax.dynamic_slice_in_dim(groups, row_start, slot_count, 1)
    text_rows = lax.dynamic_slice_in_dim(is_text, row_start, slot_count, 0)
    matched_pairs = (group_rows[:, :, None] == groups[:, None, :]) & (
        text_rows[None, :, None] != is_text[None, None, :]
    )
    layout_reward = LAYOUT_REWARD * matched_pairs.astype(jnp.float32)
    queries, all_keys, values = project(tokens, qkv_weight, query_bias, value_bias)
    query_heads = queries.reshape(doc_count, slot_count, H, head_dim)
    key_heads = all_keys.reshape(doc_count, all_slots, H, head_dim)
    value_heads = values.reshape(doc_count, all_slots, H, head_dim)
    unadjusted_scores = (
        jnp.einsum("bqhd,bkhd->bhqk", query_heads, key_heads, preferred_element_type=jnp.float32)
        * scaling
    )
    logit_scores = jnp.where(
        present_keys[:, None, None, :], unadjusted_scores + layout_reward[:, None], BLOCKED_SCORE
    )
    attn_probs, soft_pull = jax.vjp(softmax_rows, logit_scores)
    probs_low = attn_probs.astype(jnp.bfloat16)
    context = jnp.einsum(
        "bhqk,bkhd->bqhd", probs_low, value_heads, preferred_element_type=jnp.float32
    )
    context = context.reshape(row_count, features).astype(jnp.bfloat16)
    token_rows = tokens.reshape(row_count, features)
    attended = jnp.dot(context, output_weight, preferred_element_type=jnp.float32) + output_bias
    normed_one, first_pull = jax.vjp(
        layer_norm, token_rows.astype(jnp.float32) + attended, first_gain, first_shift
    )
    normed_low = normed_one.astype(jnp.bfloat16)
    inner = jnp.dot(normed_low, inner_weight, preferred_element_type=jnp.float32) + inner_bias
    activated, gate_pull = jax.vjp(smooth_gate, inner)
    hidden = activated.astype(jnp.bfloat16)
    mlp_out = jnp.dot(hidden, outer_weight, preferred_element_type=jnp.float32) + outer_bias
    layer_out, second_pull = jax.vjp(layer_norm, normed_one + mlp_out, second_gain, second_shift)
    grad_out = cotangent.reshape(row_count, features).astype(jnp.float32)
    grad_second, second_gain_grad, second_shift_grad = second_pull(grad_out)
    grad_mlp = grad_second.astype(jnp.bfloat16)
    outer_weight_grad = jnp.einsum(
        "rf,rd->fd", hidden, grad_mlp, preferred_element_type=jnp.float32
    )
    outer_bias_grad = jnp.sum(grad_mlp.astype(jnp.float32), axis=0)
    grad_hidden = jnp.einsum(
        "rd,fd->rf", grad_mlp, outer_weight, preferred_element_type=jnp.float32
    )
    grad_inner = gate_pull(grad_hidden)[0].astype(jnp.bfloat16)
    inner_weight_grad = jnp.einsum(
        "rd,rf->df", normed_low, grad_inner, preferred_element_type=jnp.float32
    )
    inner_bias_grad = jnp.sum(grad_inner.astype(jnp.float32), axis=0)
    grad_normed = grad_second + jnp.einsum(
        "rf,df->rd", grad_inner, inner_weight, preferred_element_type=jnp.float32
    )
    grad_first, first_gain_grad, first_shift_grad = first_pull(grad_normed)
    grad_attended = grad_first.astype(jnp.bfloat16)
    output_weight_grad = jnp.einsum(
        "rc,rd->cd", context, grad_attended, preferred_element_type=jnp.float32
    )
    output_bias_grad = jnp.sum(grad_attended.astype(jnp.float32), axis=0)
    grad_context = jnp.einsum(
        "rd,cd->rc", grad_attended, output_weight, preferred_element_type=jnp.float32
    )
    grad_context = grad_context.astype(jnp.bfloat16).reshape(doc_count, slot_count, H, head_dim)
    grad_probs = jnp.einsum(
        "bqhd,bkhd->bhqk", grad_context, value_heads, preferred_element_type=jnp.float32
    )
    grad_scores = soft_pull(grad_probs)[0].astype(jnp.bfloat16)
    grad_queries = (
        jnp.einsum("bhqk,bkhd->bqhd", grad_scores, key_heads, preferred_element_type=jnp.float32)
        * scaling
    )
    grad_queries = grad_queries.astype(jnp.bfloat16).reshape(row_count, features)
    key_term = (
        jnp.einsum("bhqk,bqhd->bkhd", grad_scores, query_heads, preferred_element_type=jnp.float32)
        * scaling
    )
    value_term = jnp.einsum(
        "bhqk,bqhd->bkhd", probs_low, grad_context, preferred_element_type=jnp.float32
    )
    key_sum, value_sum = (
        lax.psum_scatter(
            key_term.reshape(doc_count, all_slots, features).astype(jnp.bfloat16),
            "seq",
            scatter_dimension=1,
            tiled=True,
        ).astype(jnp.float32),
        lax.psum_scatter(
            value_term.reshape(doc_count, all_slots, features).astype(jnp.bfloat16),
            "seq",
            scatter_dimension=1,
            tiled=True,
        ).astype(jnp.float32),
    )
    grad_keys = key_sum.astype(jnp.bfloat16).reshape(row_count, features)
    grad_values = value_sum.astype(jnp.bfloat16).reshape(row_count, features)
    grad_project = jnp.concatenate([grad_queries, grad_keys, grad_values], axis=1)
    qkv_weight_grad = jnp.einsum(
        "rd,re->de", token_rows, grad_project, preferred_element_type=jnp.float32
    )
    query_bias_grad = jnp.sum(grad_queries.astype(jnp.float32), axis=0)
    value_bias_grad = jnp.sum(grad_values.astype(jnp.float32), axis=0)
    tokens_grad = grad_first + jnp.einsum(
        "re,de->rd", grad_project, qkv_weight, preferred_element_type=jnp.float32
    )
    tokens_grad = tokens_grad.astype(jnp.bfloat16).reshape(doc_count, slot_count, features)
    shares = (
        lax.psum_scatter(qkv_weight_grad, "dp", scatter_dimension=0, tiled=True),
        lax.psum_scatter(query_bias_grad, "dp", scatter_dimension=0, tiled=True),
        lax.psum_scatter(value_bias_grad, "dp", scatter_dimension=0, tiled=True),
        lax.psum_scatter(output_weight_grad, "dp", scatter_dimension=0, tiled=True),
        lax.psum_scatter(output_bias_grad, "dp", scatter_dimension=0, tiled=True),
        lax.psum_scatter(first_gain_grad, "dp", scatter_dimension=0, tiled=True),
        lax.psum_scatter(first_shift_grad, "dp", scatter_dimension=0, tiled=True),
        lax.psum_scatter(inner_weight_grad, "dp", scatter_dimension=0, tiled=True),
        lax.psum_scatter(inner_bias_grad, "dp", scatter_dimension=0, tiled=True),
        lax.psum_scatter(outer_weight_grad, "dp", scatter_dimension=0, tiled=True),
        lax.psum_scatter(outer_bias_grad, "dp", scatter_dimension=0, tiled=True),
        lax.psum_scatter(second_gain_grad, "dp", scatter_dimension=0, tiled=True),
        lax.psum_scatter(second_shift_grad, "dp", scatter_dimension=0, tiled=True),
    )
    summed = (
        lax.psum(shares[0].astype(jnp.bfloat16), "seq").astype(jnp.float32),
        lax.psum(shares[1].astype(jnp.bfloat16), "seq").astype(jnp.float32),
        lax.psum(shares[2].astype(jnp.bfloat16), "seq").astype(jnp.float32),
        lax.psum(shares[3].astype(jnp.bfloat16), "seq").astype(jnp.float32),
        lax.psum(shares[4].astype(jnp.bfloat16), "seq").astype(jnp.float32),
        lax.psum(shares[5].astype(jnp.bfloat16), "seq").astype(jnp.float32),
        lax.psum(shares[6].astype(jnp.bfloat16), "seq").astype(jnp.float32),
        lax.psum(shares[7].astype(jnp.bfloat16), "seq").astype(jnp.float32),
        lax.psum(shares[8].astype(jnp.bfloat16), "seq").astype(jnp.float32),
        lax.psum(shares[9].astype(jnp.bfloat16), "seq").astype(jnp.float32),
        lax.psum(shares[10].astype(jnp.bfloat16), "seq").astype(jnp.float32),
        lax.psum(shares[11].astype(jnp.bfloat16), "seq").astype(jnp.float32),
        lax.psum(shares[12].astype(jnp.bfloat16), "seq").astype(jnp.float32),
    )
    block_output = layer_out.astype(jnp.bfloat16).reshape(doc_count, slot_count, features)
    return (
        block_output,
        tokens_grad,
        summed[0],
        summed[1],
        summed[2],
        summed[3],
        summed[4],
        summed[5],
        summed[6],
        summed[7],
        summed[8],
        summed[9],
        summed[10],
        summed[11],
        summed[12],
    )


def solution(mesh):
    return jax.shard_map(
        local,
        mesh=mesh,
        in_specs=(
            P("dp", "seq", None),
            P("dp"),
            P("dp", None),
            P("dp", "seq", None),
            P(),
            P(),
            P(),
            P(),
            P(),
            P(),
            P(),
            P(),
            P(),
            P(),
            P(),
            P(),
            P(),
        ),
        out_specs=(
            P("dp", "seq", None),
            P("dp", "seq", None),
            P("dp", None),
            P("dp"),
            P("dp"),
            P("dp", None),
            P("dp"),
            P("dp"),
            P("dp"),
            P("dp", None),
            P("dp"),
            P("dp", None),
            P("dp"),
            P("dp"),
            P("dp"),
        ),
        check_vma=False,
    )
```

profile of v0, /device:TPU:0, one launch (start us, length us, event | category | flops | bytes accessed | tf_op | source)
XLA Modules:
  0.0 749.9 jit_solution(18409543216228144620)
XLA Ops:
  9.2 3.7 fusion.54
  16.5 3.7 fusion.14
  25.8 3.8 reshape.227
  32.1 18.9 %all-gather.5.cloned.1.call-done = bf16[2,640,768]{2,1,0:T(8,128)(2,1)} async-done(((bf16[2,320,768]{2,1,0:T(8,128)(2,1)}), bf16[2,640,768]{2,1,0:T(8,128)(2,1)}) %all-gather.5.cloned.1.call-update) | async-done | bytes 1966096 | tf_op jit(solution)/shard_map/all_gather | solution.py:55
  50.9 4.0 copy.56
  55.0 13.9 %fusion.47 = (f32[2,12,320]{2,1,0:T(8,128)}, f32[2,12,320,640]{3,2,1,0:T(8,128)}) fusion(f32[2,320,640]{2,1,0:T(8,128)} %and_select_fusion, pred[2,640]{1,0:T(4,128)(4,1)S(1)} %copy-done.20, bf16[2,640,12,64]{1,3,2,0:T(8,128)(2,1)} %bitcast.78, bf16[2,320,12,64]{1,0,3,2:T(2,128)(2,1)} %reshape.227), kind=kOutput, calls=%fused_computation.113 | convolution fusion | flops 653722240 | bytes 24280320 | tf_op jit(solution)/shard_map/jvp()/sub | solution.py:36
  70.3 11.9 %divide_convert_fusion = bf16[2,12,320,640]{3,2,1,0:T(8,128)(2,1)} fusion(f32[2,12,320,640]{3,2,1,0:T(8,128)} %get-tuple-element.103, f32[2,12,320]{2,1,0:T(8,128)} %get-tuple-element.102), kind=kLoop, calls=%fused_computation.3 | loop fusion | flops 9830400 | bytes 29521920 | tf_op jit(solution)/shard_map/convert_element_type | solution.py:105
  84.7 4.0 copy.54
  88.7 7.3 fusion.21
  105.4 24.0 %multiply_convert_fusion.1 = (bf16[640,3072]{1,0:T(8,128)(2,1)S(1)}, f32[640,3072]{1,0:T(8,128)}, f32[640,3072]{1,0:T(8,128)}) fusion(f32[3072]{0:T(1024)S(1)} %copy-done.22, bf16[768,3072]{1,0:T(8,128)(2,1)} %param.28, f32[640,768]{1,0:T(8,128)S(1)} %get-tuple-element.105, f32[768]{0:T(1024)S(1)} %copy-done.12, f32[768]{0:T(1024)S(1)} %copy-done.11, ...), kind=kOutput, calls=%fused_computation.15 | convolution fusion | flops 3152117760 | bytes 26369024 | tf_op jit(solution)/shard_map/dot_general | solution.py:116
  137.4 10.3 %convert_reduce_fusion = (f32[3072]{0:T(1024)}, bf16[640,3072]{1,0:T(8,128)(2,1)S(1)}) fusion(f32[640,3072]{1,0:T(8,128)} %get-tuple-element.98, f32[640,3072]{1,0:T(8,128)} %get-tuple-element.106, f32[3072]{0:T(1024)S(1)} %copy-done.22, bf16[640,768]{1,0:T(8,128)(2,1)S(1)} %get-tuple-element.88, bf16[3072,768]{1,0:T(8,128)(2,1)S(1)} %bitcast.86), kind=kOutput, calls=%fused_computation.13 | convolution fusion | flops 3053319168 | bytes 25387008 | tf_op jit(solution)/shard_map/rd,fd->rf/dot_general | solution.py:128
  147.8 4.3 multiply_reduce_fusion.1
  160.2 3.8 reshape.231
  164.0 7.7 %convolution_convert_fusion = bf16[2,12,64,640]{3,2,1,0:T(8,128)(2,1)} fusion(bf16[2,12,320,640]{3,2,1,0:T(8,128)(2,1)} %divide_convert_fusion, bf16[2,320,12,64]{1,0,3,2:T(2,128)(2,1)} %reshape.231), kind=kOutput, calls=%fused_computation.64 | convolution fusion | flops 630128640 | bytes 12779520 | tf_op jit(solution)/shard_map/bhqk,bqhd->bkhd/dot_general | solution.py:162
  171.7 4.1 copy.65
  175.9 16.2 %multiply_reduce_fusion = (f32[2,12,320]{2,1,0:T(8,128)S(1)}, f32[2,12,320,640]{3,2,1,0:T(8,128)}) fusion(f32[2,12,320,640]{3,2,1,0:T(8,128)} %get-tuple-element.103, f32[2,12,320]{2,1,0:T(8,128)} %multiply_divide_fusion, bf16[2,640,12,64]{1,3,2,0:T(8,128)(2,1)} %bitcast.75, bf16[2,320,12,64]{1,0,3,2:T(2,128)(2,1)} %reshape.231), kind=kOutput, calls=%fused_computation.2 | convolution fusion | flops 643883520 | bytes 42332160 | tf_op jit(solution)/shard_map/bqhd,bkhd->bhqk/dot_general | solution.py:149
  192.1 13.4 %multiply_convert_fusion = bf16[2,12,320,640]{3,2,1,0:T(8,128)(2,1)S(1)} fusion(f32[2,12,320,640]{3,2,1,0:T(8,128)} %get-tuple-element.103, f32[2,12,320,640]{3,2,1,0:T(8,128)} %get-tuple-element.111, f32[2,12,320]{2,1,0:T(8,128)S(1)} %neg.23, f32[2,12,320]{2,1,0:T(8,128)S(1)} %copy-done.10), kind=kLoop, calls=%fused_computation.1 | loop fusion | flops 19660800 | bytes 49213440 | tf_op jit(solution)/shard_map/convert_element_type | solution.py:152
  205.5 4.0 multiply_convert_fusion.2
  209.9 4.0 copy.63
  214.0 4.1 fusion.55
  218.2 11.1 %fusion.40 = f32[768,3072]{1,0:T(8,128)} fusion(bf16[640,3072]{1,0:T(8,128)(2,1)} %copy-done.7, f32[640,768]{1,0:T(8,128)} %copy-done.2, f32[768]{0:T(1024)S(1)} %copy-done.12, f32[768]{0:T(1024)S(1)} %copy-done.11, f32[640]{0:T(1024)S(1)} %fusion.34, f32[640]{0:T(1024)S(1)} %broadcast_multiply_fusion.1), kind=kOutput, calls=%fused_computation.109 | convolution fusion | flops 3022356480 | bytes 15346688 | tf_op jit(solution)/shard_map/rd,rf->df/dot_general | solution.py:132
  229.6 10.0 %fusion.56 = f32[3072,768]{1,0:T(8,128)} fusion(bf16[640,3072]{1,0:T(8,128)(2,1)} %copy-done.25, bf16[640,768]{1,0:T(8,128)(2,1)} %copy-done.8), kind=kOutput, calls=%fused_computation.118 | convolution fusion | flops 3019898880 | bytes 14352384 | tf_op jit(solution)/shard_map/rf,rd->fd/dot_general | solution.py:124
  239.6 7.4 convert_reduce_fusion.1
  257.4 8.0 %convolution_bitcast_fusion = f32[768,2304]{0,1:T(8,128)} fusion(bf16[640,768]{1,0:T(8,128)(2,1)} %bitcast.91, bf16[640,768]{0,1:T(8,128)(2,1)} %copy.67, bf16[640,768]{0,1:T(8,128)(2,1)} %copy.66, bf16[640,768]{0,1:T(8,128)(2,1)} %reshape.232), kind=kOutput, calls=%fused_computation.29 | convolution fusion | flops 2273771520 | bytes 11010048 | tf_op jit(solution)/shard_map/rd,re->de/dot_general | solution.py:182
  265.4 8.1 %copy.69 = f32[768,2304]{1,0:T(8,128)} copy(f32[768,2304]{0,1:T(8,128)} %convolution_bitcast_fusion) | data formatting | bytes 14155776
  273.8 37.0 %reduce-scatter.13.cloned.1.call-done = f32[48,768]{1,0:T(8,128)} async-done(((f32[768,768]{1,0:T(8,128)}), f32[48,768]{1,0:T(8,128)}) %reduce-scatter.13.cloned.1.call-update) | async-done | bytes 147472 | tf_op jit(solution)/shard_map/reduce_scatter | solution.py:195
  312.4 113.4 %reduce-scatter.15.cloned.1.call-done = f32[48,3072]{1,0:T(8,128)} async-done(((f32[768,3072]{1,0:T(8,128)}), f32[48,3072]{1,0:T(8,128)}) %reduce-scatter.15.cloned.1.call-update) | async-done | bytes 589840 | tf_op jit(solution)/shard_map/reduce_scatter | solution.py:199
  427.5 113.4 %reduce-scatter.17.cloned.1.call-done = f32[192,768]{1,0:T(8,128)} async-done(((f32[3072,768]{1,0:T(8,128)}), f32[192,768]{1,0:T(8,128)}) %reduce-scatter.17.cloned.1.call-update) | async-done | bytes 589840 | tf_op jit(solution)/shard_map/reduce_scatter | solution.py:201
  542.8 92.5 %reduce-scatter.19.cloned.1.call-done = f32[48,2304]{1,0:T(8,128)} async-done(((f32[768,2304]{1,0:T(8,128)}), f32[48,2304]{1,0:T(8,128)}) %reduce-scatter.19.cloned.1.call-update) | async-done | bytes 442384
  644.0 60.7 %all-reduce.10 = (bf16[768]{0:T(1024)(128)(2,1)S(1)}, bf16[768]{0:T(1024)(128)(2,1)}, bf16[768]{0:T(1024)(128)(2,1)}, bf16[768]{0:T(1024)(128)(2,1)}, bf16[768]{...) all-reduce(f32[768]{0:T(1024)} %reduce_sum.189, ...), channel_id=5, replica_groups=mesh['dp'=16,'seq'=2] {'dp'}, use_global_device_ids=true, to_apply=%region_16.17.clone | all-reduce | flops 9216 | bytes 55296
  713.8 5.7 all-reduce.11
  729.9 5.9 add_convert_fusion.1
  (152 shorter events, 93.6 us)
Async XLA Ops:
  7.2 43.7 %all-gather.5.cloned.1.call-start = ((), (), s32[]{:S(2)}) async-start(), calls=%async_computation.7 | async-start | bytes 2949120 | tf_op jit(solution)/shard_map/all_gather | solution.py:55
  9.2 7.3 copy-start.17
  9.2 7.3 copy-start.18
  16.5 68.3 %all-gather.3.cloned.1.call-start = ((), (), s32[]{:S(2)}) async-start(), calls=%async_computation.6 | async-start | bytes 2949120 | tf_op jit(solution)/shard_map/all_gather | solution.py:56
  20.3 232.5 %reduce-scatter.11.cloned.1.call-start = ((), (), s32[]{:S(2)}) async-start(), calls=%async_computation.9 | async-start | bytes 2949120 | tf_op jit(solution)/shard_map/reduce_scatter | solution.py:172
  25.8 29.2 %copy-start.20 = (pred[2,640]{1,0:T(4,128)(4,1)S(1)}, pred[2,640]{1,0:T(4,128)(4,1)}, u32[]{:S(2)}) copy-start(pred[2,640]{1,0:T(4,128)(4,1)} %iota_compare_fusion) | copy-start | bytes 3844
  96.0 5.8 copy-start.23
  101.8 3.5 copy-start.11
  101.8 3.5 copy-start.12
  101.8 3.6 copy-start.22
  101.8 27.6 %slice-start = ((s8[4718592]{0:T(1024)(128)(4,1)}), s8[4194304]{0:T(1024)(128)(4,1)S(1)}, s32[]{:S(2)}) async-start(s8[4718592]{0:T(1024)(128)(4,1)} %bitcast.85), calls=%async_computation.15 | async-start | bytes 8388608
  105.0 47.2 %copy-start.2 = (f32[640,768]{1,0:T(8,128)}, f32[640,768]{1,0:T(8,128)S(1)}, u32[]{:S(2)}) copy-start(f32[640,768]{1,0:T(8,128)S(1)} %get-tuple-element.105) | copy-start | bytes 5898244
  105.4 24.0 %slice-start.1 = ((s8[4718592]{0:T(1024)(128)(4,1)}), s8[524288]{0:T(1024)(128)(4,1)S(1)}, s32[]{:S(2)}) async-start(s8[4718592]{0:T(1024)(128)(4,1)} %bitcast.85), calls=%async_computation.16 | async-start | bytes 1048576
  105.4 24.0 %copy-start.24 = (f32[768]{0:T(1024)S(1)}, f32[768]{0:T(1024)}, u32[]{:S(2)}) copy-start(f32[768]{0:T(1024)} %param.31) | copy-start | bytes 9220
  129.4 3.9 copy-start.4
  129.4 3.9 copy-start.16
  134.8 13.0 %slice-start.2 = ((s8[4718592]{0:T(1024)(128)(4,1)}), s8[4194304]{0:T(1024)(128)(4,1)S(1)}, s32[]{:S(2)}) async-start(s8[4718592]{0:T(1024)(128)(4,1)} %bitcast.87), calls=%async_computation.17 | async-start | bytes 8388608
  137.4 10.3 %copy-start.8 = (bf16[640,768]{1,0:T(8,128)(2,1)}, bf16[640,768]{1,0:T(8,128)(2,1)S(1)}, u32[]{:S(2)}) copy-start(bf16[640,768]{1,0:T(8,128)(2,1)S(1)} %get-tuple-element.88) | copy-start | bytes 2949124
  137.4 10.3 %slice-start.3 = ((s8[4718592]{0:T(1024)(128)(4,1)}), s8[524288]{0:T(1024)(128)(4,1)S(1)}, s32[]{:S(2)}) async-start(s8[4718592]{0:T(1024)(128)(4,1)} %bitcast.87), calls=%async_computation.18 | async-start | bytes 1048576
  147.8 4.4 copy-start.7
  152.1 3.8 copy-start.21
  175.8 79.3 %reduce-scatter.9.cloned.1.call-start = ((), (), s32[]{:S(2)}) async-start(), calls=%async_computation.8 | async-start | bytes 2949120 | tf_op jit(solution)/shard_map/reduce_scatter | solution.py:166
  175.8 16.2 %copy-start.10 = (f32[2,12,320]{2,1,0:T(8,128)S(1)}, f32[2,12,320]{2,1,0:T(8,128)}, u32[]{:S(2)}) copy-start(f32[2,12,320]{2,1,0:T(8,128)} %get-tuple-element.102) | copy-start | bytes 92164
  192.1 13.4 %copy-start.3 = (bf16[2,320,12,64]{1,0,3,2:T(2,128)(2,1)S(1)}, bf16[2,320,12,64]{1,0,3,2:T(2,128)(2,1)}, u32[]{:S(2)}) copy-start(bf16[2,320,12,64]{1,0,3,2:T(2,128)(2,1)} %reshape.227) | copy-start | bytes 2949124
  205.5 4.4 copy-start.1
  214.0 96.8 %reduce-scatter.13.cloned.1.call-start = ((), (), s32[]{:S(2)}) async-start(), calls=%async_computation.10 | async-start | bytes 2506752 | tf_op jit(solution)/shard_map/reduce_scatter | solution.py:195
  218.1 207.6 %reduce-scatter.15.cloned.1.call-start = ((), (), s32[]{:S(2)}) async-start(), calls=%async_computation.11 | async-start | bytes 10027008 | tf_op jit(solution)/shard_map/reduce_scatter | solution.py:199
  229.3 311.6 %reduce-scatter.17.cloned.1.call-start = ((), (), s32[]{:S(2)}) async-start(), calls=%async_computation.12 | async-start | bytes 10027008 | tf_op jit(solution)/shard_map/reduce_scatter | solution.py:201
  239.6 395.7 %reduce-scatter.19.cloned.1.call-start = ((), (), s32[]{:S(2)}) async-start(), calls=%async_computation.13 | async-start | bytes 7520256
  273.5 370.5 %copy-start.15 = (f32[768]{0:T(1024)S(1)}, f32[768]{0:T(1024)}, u32[]{:S(2)}) copy-start(f32[768]{0:T(1024)} %get-tuple-element.62) | copy-start | bytes 9220
  273.5 456.4 %copy-start.14 = (f32[640]{0:T(1024)S(1)}, f32[640]{0:T(1024)}, u32[]{:S(2)}) copy-start(f32[640]{0:T(1024)} %copy-done.13) | copy-start | bytes 7684
  273.5 462.4 %all-reduce.15.cloned.1.call-start = ((), (), s32[]{:S(2)}) async-start(), calls=%async_computation.14 | async-start | bytes 2506752 | tf_op jit(solution)/shard_map/psum | solution.py:207
  (7 other events, 14.2 us)
Sparse Core Ops, SparseCore 0:
  16.6 34.3 all-gather.4
  53.1 31.6 all-gather.2
  175.9 30.3 reduce-scatter.10
  214.1 30.0 reduce-scatter.8
  247.8 62.9 reduce-scatter.12
  315.3 110.3 reduce-scatter.14
  429.8 111.1 reduce-scatter.16
  545.5 89.7 reduce-scatter.18
  638.9 44.5 all-reduce.14
where the time goes:
time: 754 us; the launch traced here: 750 us
  waiting for transfers between devices  378 us (50%)
  matrix products  146 us (19%)
  local copies, waits for them, and re-layouts  76.1 us (10%)
  other arithmetic  66.4 us (9%)
  blocking collectives  66.4 us (9%)
  between operations  15.8 us (2%)
    reduce_scatter x1, waiting for transfers between devices, local(): lax.psum_scatter(outer_weight_grad, 'dp', scatter_dimension=0, tiled=True)  113 us
    reduce_scatter x1, waiting for transfers between devices, local(): lax.psum_scatter(inner_weight_grad, 'dp', scatter_dimension=0, tiled=True)  113 us
    unnamed x10, waiting for transfers between devices  92.7 us
    unnamed x1, blocking collectives  60.7 us
    reduce_scatter x1, waiting for transfers between devices, local(): lax.psum_scatter(output_weight_grad, 'dp', scatter_dimension=0, tiled=True)  37 us
    unnamed x73, local copies, waits for them, and re-layouts  29.7 us
    dot_general x1, matrix products, local(): jnp.dot(normed_low, inner_weight, preferred_element_type=jnp.float32)  24 us
    all_gather x1, waiting for transfers between devices, project(): lax.all_gather(own_keys, 'seq', axis=1, tiled=True)  18.9 us
  transfers between devices with their start and end apart: 9, of which 6 were waited for; matrix products, arithmetic and copies ran while one was open for 24% of the time, Pallas kernels for 0%

commit v1 on v0

--- a/solution.py
+++ b/solution.py
@@ -1,6 +1,10 @@
+import functools
+
 import jax
 import jax.numpy as jnp
 from jax import lax
+from jax.experimental import pallas as pl
+from jax.experimental.pallas import tpu as pltpu
 from jax.sharding import PartitionSpec as P
 
 H = 12
@@ -9,6 +13,683 @@
 LAYOUT_REWARD = 2.0
 BLOCKED_SCORE = -1000000000.0
 NORM_EPS = 1e-05
+LOG2E = 1.4426950408889634
+HEAD = 64
+PAIR = 128
+WIDE = 256
+BF, F32 = jnp.bfloat16, jnp.float32
+
+
+def dot(left, right):
+    return jnp.dot(left, right, preferred_element_type=F32)
+
+
+def dot_nt(left, right):
+    return lax.dot_general(left, right, (((1,), (1,)), ((), ())), preferred_element_type=F32)
+
+
+def dot_tn(left, right):
+    return lax.dot_general(left, right, (((0,), (0,)), ((), ())), preferred_element_type=F32)
+
+
+def at(start, size):
+    return pl.ds(pl.multiple_of(start, size), size)
+
+
+def loop(count, body):
+    def step(index, carry):
+        body(index)
+        return carry
+
+    lax.fori_loop(0, count, step, 0)
+
+
+def fold_rows(block):
+    rows, columns = block.shape
+    return jnp.sum(block.reshape(rows // 8, 8, columns), axis=0)
+
+
+def project_tokens(x, w_qkv, bias_row, qkv, rows):
+    columns = w_qkv.shape[1]
+
+    def body(index):
+        here = at(index * WIDE, WIDE)
+        qkv[rows, here] = (dot(x[rows, :], w_qkv[:, here]) + bias_row[0:1, here]).astype(BF)
+
+    loop(columns // WIDE, body)
+
+
+def fill_reward(reward, seg_row, count):
+    text = seg_row.shape[1]
+    segs = reward.shape[0] - text
+    key = lax.broadcasted_iota(jnp.int32, (segs, text), 0)
+    match = jnp.where(key == seg_row, LAYOUT_REWARD * LOG2E, 0.0).astype(F32)
+    dead = jnp.where(key >= count, BLOCKED_SCORE * LOG2E, 0.0).astype(F32)
+    turned = jnp.transpose(match)
+    reward[...] = jnp.zeros_like(reward)
+    slots = text + segs
+    for head in range(2):
+        reward[text:slots, head * slots : head * slots + text] = match + dead
+        reward[text:slots, head * slots + text : (head + 1) * slots] = dead[:, :segs]
+        reward[0:text, head * slots + text : (head + 1) * slots] = turned
+
+
+def split_heads(block, both):
+    slots = block.shape[0]
+    first = lax.broadcasted_iota(jnp.int32, block.shape, 1) < HEAD
+    zero = jnp.zeros_like(block)
+    both[0:slots, :] = jnp.where(first, block, zero)
+    both[slots:, :] = jnp.where(first, zero, block)
+
+
+def attend(qkv, reward, probs_of, context_t, both, turned, side):
+    slots, features = qkv.shape[0], qkv.shape[1] // 3
+    pairs = features // PAIR
+    scaling = HEAD ** (-0.5) * LOG2E
+
+    def pair_step(pair):
+        here = at(pair * PAIR, PAIR)
+        keys = qkv[:, at(features + pair * PAIR, PAIR)]
+        split_heads(qkv[:, here], both)
+        turned[...] = jnp.transpose(qkv[:, at(2 * features + pair * PAIR, PAIR)])
+        probs = probs_of(pair)
+
+        for chunk in range(2 * slots // WIDE):
+            block = slice(chunk * WIDE, (chunk + 1) * WIDE)
+            scores = dot_nt(keys, both[block, :]) * scaling + reward[:, block]
+            scores = jnp.exp2(scores - jnp.max(scores, axis=0, keepdims=True))
+            low = (scores * (1.0 / jnp.sum(scores, axis=0, keepdims=True))).astype(BF)
+            probs[:, block] = low
+            side[:, block] = dot(turned[...], low).astype(BF)
+        context_t[at(pair * PAIR, HEAD), :] = side[:HEAD, :slots]
+        context_t[at(pair * PAIR + HEAD, HEAD), :] = side[HEAD:, slots:]
+
+    return pair_step, pairs
+
+
+def first_norm(x, attended, bias, gain, shift, normal, root, low, rows):
+    def body(index):
+        here = at(index * rows, rows)
+        hidden = x[here, :].astype(F32) + (attended[here, :] + bias[...])
+        centre = hidden - jnp.mean(hidden, axis=1, keepdims=True)
+        inverse = lax.rsqrt(jnp.mean(centre * centre, axis=1, keepdims=True) + NORM_EPS)
+        unit = centre * inverse
+        normal[here, :] = unit
+        root[here, :] = jnp.broadcast_to(inverse, (rows, PAIR))
+        low[here, :] = (unit * gain[...] + shift[...]).astype(BF)
+
+    loop(x.shape[0] // rows, body)
+
+
+def gate(inner):
+    normal = 0.5 * (1.0 + lax.erf(inner * 0.7071067811865476))
+    density = jnp.exp2(inner * inner * (-0.5 * LOG2E)) * 0.3989422804014327
+    return inner * normal, normal + inner * density
+
+
+def feed_forward(low, w_inner, b_inner, hidden, slope):
+    def body(index):
+        here = at(index * WIDE, WIDE)
+        value, grade = gate(dot(low[...], w_inner[:, here]) + b_inner[0:1, here])
+        hidden[:, here] = value.astype(BF)
+        slope[:, here] = grade.astype(BF)
+
+    loop(w_inner.shape[1] // WIDE, body)
+
+
+def second_norm(normal, first_gain, first_shift, mlp, bias, gain, shift, cotangent, output, grad, grad_low, sums, rows):
+    sums[0:3] = jnp.zeros((3,) + sums.shape[1:], F32)
+
+    def body(index):
+        here = at(index * rows, rows)
+        one = normal[here, :] * first_gain[...] + first_shift[...]
+        total = one + (mlp[here, :] + bias[...])
+        centre = total - jnp.mean(total, axis=1, keepdims=True)
+        inverse = lax.rsqrt(jnp.mean(centre * centre, axis=1, keepdims=True) + NORM_EPS)
+        unit = centre * inverse
+        pull = cotangent[here, :].astype(F32)
+        output[here, :] = (unit * gain[...] + shift[...]).astype(BF)
+        scaled = pull * gain[...]
+        back = inverse * (
+            scaled
+            - jnp.mean(scaled, axis=1, keepdims=True)
+            - unit * jnp.mean(scaled * unit, axis=1, keepdims=True)
+        )
+        rounded = back.astype(BF)
+        grad[here, :] = back
+        grad_low[here, :] = rounded
+        sums[0] += fold_rows(pull * unit)
+        sums[1] += fold_rows(pull)
+        sums[2] += fold_rows(rounded.astype(F32))
+
+    loop(normal.shape[0] // rows, body)
+
+
+def first_norm_back(grad_second, back, normal, root, gain, grad_first, grad_low, sums, rows):
+    sums[3:6] = jnp.zeros((3,) + sums.shape[1:], F32)
+
+    def body(index):
+        here = at(index * rows, rows)
+        pull = grad_second[here, :] + back[here, :]
+        unit = normal[here, :]
+        scaled = pull * gain[...]
+        inverse = root[here, 0:1]
+        first = inverse * (
+            scaled
+            - jnp.mean(scaled, axis=1, keepdims=True)
+            - unit * jnp.mean(scaled * unit, axis=1, keepdims=True)
+        )
+        rounded = first.astype(BF)
+        grad_first[here, :] = first
+        grad_low[here, :] = rounded
+        sums[3] += fold_rows(pull * unit)
+        sums[4] += fold_rows(pull)
+        sums[5] += fold_rows(rounded.astype(F32))
+
+    loop(normal.shape[0] // rows, body)
+
+
+def attend_back(qkv, grad_context, probs_of, grad_qkv, both, both_grad, turned, scores, side, points):
+    slots, features = qkv.shape[0], qkv.shape[1] // 3
+    scaling = HEAD ** (-0.5)
+
+    def pair_step(pair):
+        here = at(pair * PAIR, PAIR)
+        there = at(features + pair * PAIR, PAIR)
+        last = at(2 * features + pair * PAIR, PAIR)
+        split_heads(qkv[:, here], both)
+        split_heads(grad_context[:, here], both_grad)
+        turned[...] = jnp.transpose(qkv[:, there])
+        values = qkv[:, last]
+        probs = probs_of(pair)
+        for chunk in range(2 * slots // WIDE):
+            block = slice(chunk * WIDE, (chunk + 1) * WIDE)
+            pull = dot_nt(values, both_grad[block, :])
+            weight = probs[:, block].astype(F32)
+            mean = jnp.sum(weight * pull, axis=0, keepdims=True)
+            low = (weight * (pull - mean)).astype(BF)
+            scores[:, block] = low
+            side[:, block] = dot(turned[...], low)
+            if chunk == 2:
+                points("u", pair)
+        points("v", pair)
+        grad_qkv[:, there] = (dot(scores[...], both[...]) * scaling).astype(BF)
+        grad_qkv[:, last] = dot(probs[...], both_grad[...]).astype(BF)
+        mine = jnp.concatenate([side[:HEAD, :slots], side[HEAD:, slots:]], axis=0)
+        grad_qkv[:, here] = jnp.transpose(mine * scaling).astype(BF)
+
+    return pair_step, features // PAIR
+
+
+PARTS = 16
+MESH = pl.DeviceIdType.MESH
+UNIT_ROWS = 48
+UNITS = 12
+WEIGHT = {"c": 1, "y": 2, "l": 4, "h": 8}
+ORDERS = ("cyxlhg", "clyhxg")
+SMALL_ORDER = "cylhx"
+SWAP = 0
+
+
+def partner_of(bit, me, seq):
+    if bit in "xg":
+        return (me, 1 - seq)
+    weight = WEIGHT[bit]
+    return (me + weight * (1 - 2 * ((me // weight) % 2)), seq)
+
+
+def stage_shapes(order, rows, columns):
+    bits, shapes = 4, []
+    for bit in order:
+        if bit == "x":
+            columns //= 2
+        elif bit != "g":
+            bits -= 1
+        shapes.append((2,) * bits + (rows, columns))
+    return shapes
+
+
+def add_into(target, other):
+    lead = target.shape[:-2]
+    total = 1
+    for size in lead:
+        total *= size
+
+    def step(index, carry):
+        place, rest = [], index
+        for size in reversed(lead):
+            place.append(rest % size)
+            rest = rest // size
+        place = tuple(reversed(place)) + (slice(None), slice(None))
+        target[place] = (target[place].astype(F32) + other[place].astype(F32)).astype(BF)
+        return carry
+
+    if total == 1:
+        step(0, 0)
+    else:
+        lax.fori_loop(0, total, step, 0)
+
+
+class Unit:
+    def __init__(self, number, source, order, buffers, sends, recvs, me, seq):
+        self.number, self.source, self.order, self.buffers = number, source, order, buffers
+        self.sends, self.recvs, self.me, self.seq = sends, recvs, me, seq
+
+    def at_stage(self, stage):
+        bits = ["h", "l", "y", "c"]
+        for bit in self.order[:stage]:
+            if bit in bits:
+                bits.remove(bit)
+        current = self.buffers[stage - 1] if stage else self.source
+        bit = self.order[stage]
+        if bit == "g":
+            return current, None
+        if bit == "x":
+            size = current.shape[-1] // 2
+            lead = (slice(None),) * (len(bits) + 1)
+            own = current.at[lead + (pl.ds(pl.multiple_of(self.seq * size, PAIR), size),)]
+            return current.at[lead + (pl.ds(pl.multiple_of((1 - self.seq) * size, PAIR), size),)], own
+        mine = (self.me // WEIGHT[bit]) % 2
+        lead = (slice(None),) * bits.index(bit)
+        return current.at[lead + (1 - mine,)], current.at[lead + (mine,)]
+
+    def copy(self, stage):
+        return pltpu.make_async_remote_copy(
+            src_ref=self.at_stage(stage)[0],
+            dst_ref=self.buffers[stage],
+            send_sem=self.sends.at[self.number, stage],
+            recv_sem=self.recvs.at[self.number, stage],
+            device_id=partner_of(self.order[stage], self.me, self.seq),
+            device_id_type=MESH,
+        )
+
+    def advance(self, stage):
+        self.copy(stage).wait()
+        self.add(stage)
+
+    def add(self, stage):
+        kept = self.at_stage(stage)[1]
+        if kept is not None:
+            add_into(self.buffers[stage], kept)
+        if stage + 1 < len(self.order):
+            self.copy(stage + 1).start()
+
+
+def with_stages(schedule):
+    reached = [0] * (UNITS + 1)
+    plan = {}
+    for point, numbers in schedule:
+        steps = plan.setdefault(point, [])
+        for number in numbers:
+            steps.append((number, reached[number]))
+            reached[number] += 1
+    return plan
+
+
+def layer_kernel(
+    tokens, cotangent, seg_align, seg_count, vectors, w_qkv, w_out, w_inner, w_outer,
+    block_output, tokens_grad, g_qkv, g_out, g_inner, g_outer, sums_out, probs_hbm,
+    x, qkv, context_t, w_out_v, normal, root, cot, acc, grad_att, sums, own, small, small_got, *rest,
+):
+    rest = list(rest)
+    buffers = [[rest.pop(0) for _ in ORDERS[0]] for _ in range(UNITS)]
+    unit_send, unit_recv, outer_send, outer_recv, local_sem, pair_sem, swap_send, swap_recv, small_send, small_recv = rest
+    slots, features = x.shape
+    half = slots // 2
+    wide = w_inner.shape[1]
+    me, seq = lax.axis_index("dp"), lax.axis_index("seq")
+    core = me % 2
+    mine, other = at(seq * half, half), at((1 - seq) * half, half)
+    b_out, gain1, shift1, b_outer, gain2, shift2 = (vectors.at[i : i + 1] for i in range(3, 9))
+    columns = [slice(c * WIDE, (c + 1) * WIDE) for c in range(features // WIDE)]
+
+    barrier = pltpu.get_barrier_semaphore()
+    for bit in "xcylh":
+        pl.semaphore_signal(barrier, inc=1, device_id=partner_of(bit, me, seq), device_id_type=MESH)
+
+    def local(source, target, index):
+        return pltpu.make_async_copy(source, target, local_sem.at[index])
+
+    def swap(source, target, index):
+        return pltpu.make_async_remote_copy(
+            src_ref=source, dst_ref=target, send_sem=swap_send.at[index], recv_sem=swap_recv.at[index],
+            device_id=(me, 1 - seq), device_id_type=MESH)
+
+    keep_tokens = local(tokens.at[seq], x.at[mine], 0)
+    keep_cot = local(cotangent.at[seq], cot.at[mine], 1)
+    load_out = local(w_out, w_out_v, 2)
+    swap_tokens = swap(tokens.at[1 - seq], x.at[mine], 0)
+    swap_cot = swap(cotangent.at[1 - seq], cot.at[mine], 1)
+    keep_output = local(cot.at[mine], block_output.at[seq], 3)
+    swap_output = swap(cot.at[other], block_output.at[seq], 2)
+    keep_grad = local(x.at[mine], tokens_grad.at[seq], 4)
+    swap_grad = swap(x.at[other], tokens_grad.at[seq], 3)
+    keep_tokens.start()
+
+    units = [
+        Unit(n, own.at[n if n < 8 else n - 8], ORDERS[n % 2], buffers[n], unit_send, unit_recv, me, seq)
+        for n in range(UNITS)
+    ]
+
+    def outer_copy(j, sub):
+        hi, lo = j // 2, j % 2
+        return pltpu.make_async_remote_copy(
+            src_ref=own.at[sub, hi, lo, :, 1 - core],
+            dst_ref=buffers[sub][0].at[hi, lo],
+            send_sem=outer_send.at[j, sub], recv_sem=outer_recv.at[j, sub],
+            device_id=partner_of("c", me, seq), device_id_type=MESH)
+
+    def small_copy(stage):
+        return pltpu.make_async_remote_copy(
+            src_ref=small, dst_ref=small_got.at[stage], send_sem=small_send.at[stage], recv_sem=small_recv.at[stage],
+            device_id=partner_of(SMALL_ORDER[stage], me, seq), device_id_type=MESH)
+
+    def advance(number, stage):
+        if number == UNITS:
+            small_copy(stage).wait()
+            small[...] += small_got[stage]
+            if stage + 1 < len(SMALL_ORDER):
+                small_copy(stage + 1).start()
+        elif number < 4 and stage == 0:
+            for j in range(4):
+                outer_copy(j, number).wait()
+            units[number].add(0)
+        else:
+            units[number].advance(stage)
+
+    plan = with_stages(SCHEDULE)
+
+    def point(name):
+        for number, stage in plan.get(name, ()):
+            advance(number, stage)
+
+    def points(name, index, count):
+        for i in range(count):
+            if (name, i) in plan:
+                pl.when(index == i)(functools.partial(point, (name, i)))
+
+    def forward(w_inner_v, w_outer_v):
+        load_inner, load_outer = local(w_inner, w_inner_v, 5), local(w_outer, w_outer_v, 6)
+
+        def attention(w_qkv_v, reward, both, turned, side, probs_buf):
+            load_qkv = local(w_qkv, w_qkv_v, 7)
+            load_qkv.start()
+            pl.semaphore_wait(barrier, 5)
+            swap_tokens.start()
+            load_out.start()
+            fill_reward(reward, seg_align[pl.ds(seq, 1), :], seg_count[seq])
+            keep_tokens.wait()
+            load_qkv.wait()
+
+            def project(rows):
+                def body(index):
+                    here = at(index * WIDE, WIDE)
+                    bias = vectors[pl.ds(index // 3, 1), at(index % 3 * WIDE, WIDE)]
+                    qkv[rows, here] = (dot(x[rows, :], w_qkv_v[:, here]) + bias).astype(BF)
+
+                loop(3 * features // WIDE, body)
+
+            project(mine)
+            load_inner.start()
+            load_outer.start()
+            keep_cot.start()
+            swap_tokens.wait()
+            swap_cot.start()
+            project(other)
+            step, pairs = attend(qkv, reward, lambda pair: probs_buf.at[pair % 2], context_t, both, turned, side)
+
+            def out_copy(pair):
+                return pltpu.make_async_copy(probs_buf.at[pair % 2], probs_hbm.at[pair], pair_sem.at[pair % 2])
+
+            def body(pair):
+                @pl.when(pair >= 2)
+                def _():
+                    out_copy(pair - 2).wait()
+
+                step(pair)
+                out_copy(pair).start()
+
+            loop(pairs, body)
+            out_copy(pairs - 2).wait()
+            out_copy(pairs - 1).wait()
+
+        pl.run_scoped(
+            attention,
+            pltpu.VMEM((features, 3 * features), BF),
+            pltpu.VMEM((slots, 2 * slots), F32),
+            pltpu.VMEM((2 * slots, PAIR), BF),
+            pltpu.VMEM((PAIR, slots), BF),
+            pltpu.VMEM((PAIR, 2 * slots), BF),
+            pltpu.VMEM((2, slots, 2 * slots), BF),
+        )
+
+        def mlp(low, turned_low, hidden, slope, grad_second):
+            low[...] = jnp.transpose(context_t[...])
+            load_out.wait()
+            for here in columns:
+                acc[:, here] = dot(low[...], w_out_v[:, here])
+            first_norm(x, acc, b_out, gain1, shift1, normal, root, low, 32)
+            load_inner.wait()
+
+            def inner_body(index):
+                here = at(index * WIDE, WIDE)
+                bias = vectors[pl.ds(9 + index // 3, 1), at(index % 3 * WIDE, WIDE)]
+                value, grade = gate(dot(low[...], w_inner_v[:, here]) + bias)
+                hidden[:, here] = value.astype(BF)
+                slope[:, here] = grade.astype(BF)
+
+            loop(wide // WIDE, inner_body)
+            load_outer.wait()
+            for here in columns:
+                acc[:, here] = dot(hidden[...], w_outer_v[:, here])
+            keep_cot.wait()
+            swap_cot.wait()
+            second_norm(normal, gain1, shift1, acc, b_outer, gain2, shift2, cot, cot, grad_second, grad_att, sums, 32)
+            keep_output.start()
+            swap_output.start()
+            turned_low[...] = jnp.transpose(low[...])
+
+            def outer_step(j):
+                block = dot_tn(hidden[:, at(j * features, features)], grad_att[...]).astype(BF)
+                block = block.reshape(2, 2, 4, UNIT_ROWS, features)
+                for sub in range(4):
+                    own[sub, j // 2, j % 2] = block[:, :, sub]
+                for sub in range(4):
+                    outer_copy(j, sub).start()
+
+            loop(4, outer_step)
+
+            def inner_step(j):
+                here = at(j * features, features)
+                low_grad = (
+                    dot_nt(grad_att[...], w_outer_v[here, :]) * slope[:, here].astype(F32)
+                ).astype(BF)
+                hidden[:, here] = low_grad
+                sums[8 + j] = fold_rows(low_grad.astype(F32))
+                points("g", j, 4)
+                block = dot(turned_low[...], hidden[:, here]).astype(BF)
+                own[4 + j] = block.reshape(2, 2, 2, 2, UNIT_ROWS, features)
+                for i in range(4):
+                    pl.when(j == i)(lambda i=i: units[4 + i].copy(0).start())
+                points("i", j, 4)
+
+            loop(4, inner_step)
+            for c, here in enumerate(columns):
+                acc[:, here] = dot_nt(hidden[...], w_inner_v[here, :])
+                point(("a", c))
+            first_norm_back(grad_second, acc, normal, root, gain1, acc, grad_att, sums, 32)
+
+        pl.run_scoped(
+            mlp,
+            pltpu.VMEM((slots, features), BF),
+            pltpu.VMEM((features, slots), BF),
+            pltpu.VMEM((slots, wide), BF),
+            pltpu.VMEM((slots, wide), BF),
+            pltpu.VMEM((slots, features), F32),
+        )
+
+    pl.run_scoped(forward, pltpu.VMEM(w_inner.shape, BF), pltpu.VMEM(w_outer.shape, BF))
+
+    def back(w_qkv_v, both, both_grad, turned, scores, side, probs_buf, grad_ctx, grad_qkv, turned_x):
+        load_qkv = local(w_qkv, w_qkv_v, 8)
+        load_qkv.start()
+
+        def in_copy(pair):
+            return pltpu.make_async_copy(probs_hbm.at[pair], probs_buf.at[pair % 2], pair_sem.at[pair % 2])
+
+        in_copy(0).start()
+        point(("n", 0))
+        for c, here in enumerate(columns):
+            block = dot(context_t[...], grad_att[:, here]).astype(BF)
+            own[0, :, :, :, :, :, here] = block.reshape(2, 2, 2, 2, UNIT_ROWS, WIDE)
+        units[8].copy(0).start()
+        point(("o", 0))
+        for c, here in enumerate(columns):
+            grad_ctx[:, here] = dot_nt(grad_att[...], w_out_v[here, :]).astype(BF)
+        turned_x[...] = jnp.transpose(x[...])
+        point(("o", 1))
+        step, pairs = attend_back(
+            qkv, grad_ctx, lambda pair: probs_buf.at[pair % 2], grad_qkv, both, both_grad, turned, scores, side,
+            lambda name, pair: points(name, pair, pairs))
+
+        def body(pair):
+            @pl.when(pair + 1 < pairs)
+            def _():
+                in_copy(pair + 1).start()
+
+            in_copy(pair).wait()
+            step(pair)
+            points("r", pair, pairs)
+
+            @pl.when(pair % 2 == 1)
+            def _():
+                group = pair // 2
+                for part in range(3):
+                    there = at(part * features + group * WIDE, WIDE)
+                    block = dot(turned_x[...], grad_qkv[:, there]).astype(BF)
+                    own[1 + group, :, :, :, :, :, part * WIDE : (part + 1) * WIDE] = block.reshape(
+                        2, 2, 2, 2, UNIT_ROWS, WIDE)
+                for i in range(3):
+                    pl.when(group == i)(lambda i=i: units[9 + i].copy(0).start())
+
+            points("s", pair, pairs)
+
+        loop(pairs, body)
+        sums[6] = fold_rows(grad_qkv[:, :features].astype(F32))
+        sums[7] = fold_rows(grad_qkv[:, 2 * features :].astype(F32))
+        small[...] = jnp.sum(sums[...], axis=1)
+        small_copy(0).start()
+        load_qkv.wait()
+        for side_index, rows in enumerate((other, mine)):
+            for c, here in enumerate(columns):
+                x[rows, here] = (acc[rows, here] + dot_nt(grad_qkv[rows, :], w_qkv_v[here, :])).astype(BF)
+                point(("t", side_index * 3 + c))
+            (swap_grad if side_index == 0 else keep_grad).start()
+
+    pl.run_scoped(
+        back,
+        pltpu.VMEM((features, 3 * features), BF),
+        pltpu.VMEM((2 * slots, PAIR), BF),
+        pltpu.VMEM((2 * slots, PAIR), BF),
+        pltpu.VMEM((PAIR, slots), BF),
+        pltpu.VMEM((slots, 2 * slots), BF),
+        pltpu.VMEM((PAIR, 2 * slots), F32),
+        pltpu.VMEM((2, slots, 2 * slots), BF),
+        pltpu.VMEM((slots, features), BF),
+        pltpu.VMEM((slots, 3 * features), BF),
+        pltpu.VMEM((features, slots), BF),
+    )
+    point(("end", 0))
+    keep_output.wait()
+    swap_output.wait()
+    keep_grad.wait()
+    swap_grad.wait()
+    sums_out[...] = small[...]
+    size = features // 2
+    for number in range(UNITS):
+        kept, got = (buffers[number][stage] for stage in (4, 5))
+        for side in range(2):
+
+            @pl.when(seq == side)
+            def _():
+                for block, place in ((kept, side), (got, 1 - side)):
+                    value = block[...].astype(F32)
+                    start = place * size
+                    if number < 4:
+                        g_outer[number * UNIT_ROWS : (number + 1) * UNIT_ROWS, start : start + size] = value
+                    elif number < 8:
+                        start += (number - 4) * features
+                        g_inner[:, start : start + size] = value
+                    elif number == 8:
+                        g_out[:, start : start + size] = value
+                    else:
+                        for piece in range(size // PAIR):
+                            column = start + piece * PAIR
+                            target = column // WIDE * features + (number - 9) * WIDE + column % WIDE
+                            g_qkv[:, target : target + PAIR] = value[:, piece * PAIR : (piece + 1) * PAIR]
+
+
+def layer(tokens, cotangent, seg_align, seg_count, vectors, w_qkv, w_out, w_inner, w_outer):
+    documents, half, features = tokens.shape
+    slots, wide = 2 * half, w_inner.shape[1]
+    pairs = features // PAIR
+    S, V, D = jax.ShapeDtypeStruct, pltpu.VMEM, pltpu.SemaphoreType.DMA
+    scratch = [
+        V((slots, features), BF), V((slots, 3 * features), BF), V((features, slots), BF), V(w_out.shape, BF),
+        V((slots, features), F32), V((slots, PAIR), F32), V((slots, features), BF), V((slots, features), F32),
+        V((slots, features), BF), V((16, 8, features), F32), V((8, 2, 2, 2, 2, UNIT_ROWS, features), BF),
+        V((16, features), F32), V((len(SMALL_ORDER), 16, features), F32),
+    ]
+    for number in range(UNITS):
+        scratch += [V(shape, BF) for shape in stage_shapes(ORDERS[number % 2], UNIT_ROWS, features)]
+    scratch += [D((UNITS, 6)), D((UNITS, 6)), D((4, 4)), D((4, 4)), D((9,)), D((2,)), D((4,)), D((4,)), D((5,)), D((5,))]
+    hbm, vmem = pl.BlockSpec(memory_space=pltpu.HBM), pl.BlockSpec(memory_space=pltpu.VMEM)
+    return pl.pallas_call(
+        layer_kernel,
+        name="layer",
+        out_shape=[
+            S(tokens.shape, BF), S(tokens.shape, BF), S((UNIT_ROWS, 3 * features), F32), S((UNIT_ROWS, features), F32),
+            S((UNIT_ROWS, wide), F32), S((4 * UNIT_ROWS, features), F32), S((16, features), F32),
+            S((pairs, slots, 2 * slots), BF),
+        ],
+        in_specs=[hbm, hbm, vmem, pl.BlockSpec(memory_space=pltpu.SMEM), vmem, hbm, hbm, hbm, hbm],
+        out_specs=[hbm, hbm, vmem, vmem, vmem, vmem, vmem, hbm],
+        scratch_shapes=scratch,
+        compiler_params=pltpu.CompilerParams(collective_id=0, has_side_effects=True, vmem_limit_bytes=60 * 2**20),
+    )(tokens, cotangent, seg_align, seg_count, vectors, w_qkv, w_out, w_inner, w_outer)
+
+
+SCHEDULE = (
+    (("i", 1), (0,)),
+    (("g", 2), (1,)),
+    (("i", 2), (2,)),
+    (("g", 3), (3,)),
+    (("i", 3), (4,)),
+    (("a", 0), (5,)),
+    (("a", 1), (0, 6)),
+    (("a", 2), (1, 7)),
+    (("n", 0), (2,)),
+    (("o", 0), (0,)),
+    (("o", 1), (3,)),
+    (("v", 0), (8, 4, 2)),
+    (("r", 0), (5,)),
+    (("s", 1), (6, 4)),
+    (("u", 2), (7,)),
+    (("v", 2), (1, 0)),
+    (("r", 2), (2,)),
+    (("u", 3), (9, 3, 4, 6)),
+    (("s", 3), (1,)),
+    (("u", 4), (0, 8)),
+    (("v", 4), (2,)),
+    (("r", 4), (1,)),
+    (("u", 5), (10, 5, 0)),
+    (("r", 5), (9, 7, 8)),
+    (("s", 5), (2, 1)),
+    (("t", 0), (3,)),
+    (("t", 2), (4,)),
+    (("t", 4), (6,)),
+    (("end", 0), (11, 12, 3, 10, 4, 5, 9, 12, 7, 8, 6, 11, 3, 12, 9, 10, 8, 5, 11, 7, 12, 6, 9, 10, 8, 5, 7, 12, 11, 9, 10, 11, 10, 11)),
+)
 
 
 def slot_groups(seg_count, seg_align, all_slots):
@@ -58,7 +739,7 @@
     return (queries, all_keys, values)
 
 
-def local(
+def plain(
     tokens,
     seg_count,
     seg_align,
@@ -238,6 +919,71 @@
     )
 
 
+def local(
+    tokens,
+    seg_count,
+    seg_align,
+    cotangent,
+    qkv_weight,
+    query_bias,
+    value_bias,
+    output_weight,
+    output_bias,
+    first_gain,
+    first_shift,
+    inner_weight,
+    inner_bias,
+    outer_weight,
+    outer_bias,
+    second_gain,
+    second_shift,
+):
+    dp, seq = lax.axis_size("dp"), lax.axis_size("seq")
+    documents, _, features = tokens.shape
+    if dp != PARTS or seq != 2 or documents != 2 or features != PARTS * UNIT_ROWS:
+        return plain(
+            tokens, seg_count, seg_align, cotangent, qkv_weight, query_bias, value_bias, output_weight, output_bias, first_gain, first_shift, inner_weight, inner_bias, outer_weight, outer_bias, second_gain, second_shift
+        )
+    vectors = jnp.concatenate(
+        [
+            query_bias,
+            jnp.zeros_like(query_bias),
+            value_bias,
+            output_bias,
+            first_gain,
+            first_shift,
+            outer_bias,
+            second_gain,
+            second_shift,
+            inner_bias,
+            jnp.zeros((3 * features,), F32),
+        ]
+    ).reshape(16, features)
+    block_output, tokens_grad, g_qkv, g_out, g_inner, g_outer, sums, _ = layer(
+        tokens, cotangent, seg_align, seg_count, vectors, qkv_weight, output_weight, inner_weight, outer_weight
+    )
+    place = lax.axis_index("dp")
+    rows = lax.dynamic_slice(sums, (0, place * UNIT_ROWS), (8, UNIT_ROWS))
+    inner_bias_grad = lax.dynamic_slice(sums[8:12].reshape(-1), (place * 4 * UNIT_ROWS,), (4 * UNIT_ROWS,))
+    return (
+        block_output,
+        tokens_grad,
+        g_qkv,
+        rows[6],
+        rows[7],
+        g_out,
+        rows[5],
+        rows[3],
+        rows[4],
+        g_inner,
+        inner_bias_grad,
+        g_outer,
+        rows[2],
+        rows[0],
+        rows[1],
+    )
+
+
 def solution(mesh):
     return jax.shard_map(
         local,

time: 754 us -> 178 us (0.24)
  waiting for transfers between devices: 378 us -> 0 us
  Pallas kernels: 0 us -> 159 us
  matrix products: 146 us -> 0 us
  blocking collectives: 66.4 us -> 0 us
  other arithmetic: 66.4 us -> 0.01 us
  local copies, waits for them, and re-layouts: 76.1 us -> 18.2 us
  between operations: 15.8 us -> 0.7 us
    reduce_scatter x5 -> x0, waiting for transfers between devices: 264 us -> none  [the longest x1 113 us: local(): lax.psum_scatter(outer_weight_grad, 'dp', scatter_dimension=0, tiled=True)]
    pallas_call x0 -> x1, Pallas kernels: none -> 159 us  [layer(): pl.pallas_call(layer_kernel, name='layer', out_shape=[S(tokens.shape, BF)...]
    dot_general x17 -> x0, matrix products: 132 us -> none  [the longest x1 24 us: local(): jnp.dot(normed_low, inner_weight, preferred_element_type=jnp.float32)]
    unnamed x10 -> x0, waiting for transfers between devices: 92.7 us -> none
    unnamed x1 -> x0, blocking collectives: 60.7 us -> none
    convert_element_type x18 -> x0, other arithmetic: 49.8 us -> none  [the longest x1 13.4 us: local(): grad_scores = soft_pull(grad_probs)[0].astype(jnp.bfloat16)]
    all_gather x2 -> x0, waiting for transfers between devices: 21.3 us -> none  [the longest x1 18.9 us: project(): lax.all_gather(own_keys, 'seq', axis=1, tiled=True)]
    convert_element_type x7 -> x0, local copies, waits for them, and re-layouts: 20.8 us -> none  [the longest x2 5.78 us: local(): context = context.reshape(row_count, features).astype(jnp.bfloat16)]
  transfers between devices with their start and end apart: 9 -> 0, of which waited for: 6 -> 0; matrix products, arithmetic and copies ran while one was open for 24% -> 0% of each run, Pallas kernels for 0% -> 0%
where the time goes in v1:
time: 178 us
  Pallas kernels  159 us (89%)
  local copies, waits for them, and re-layouts  18.2 us (10%)
    pallas_call x1, Pallas kernels, layer(): pl.pallas_call(layer_kernel, name='layer', out_shape=[S(tokens.shape, BF)...  159 us
    unnamed x22, local copies, waits for them, and re-layouts  14.8 us

profile of v1, /device:TPU:0, one launch (start us, length us, event | category | flops | bytes accessed | tf_op | source)
XLA Modules:
  0.0 177.6 jit_solution(10517520909433459719)
XLA Ops:
  0.7 0.7 constant_dynamic-update-slice_fusion.9
  1.4 0.7 constant_dynamic-update-slice_fusion.7
  2.0 0.7 constant_dynamic-update-slice_fusion.6
  2.7 0.7 constant_dynamic-update-slice_fusion.5
  3.4 0.7 constant_dynamic-update-slice_fusion.4
  4.1 0.7 constant_dynamic-update-slice_fusion.3
  4.8 0.7 constant_dynamic-update-slice_fusion.2
  5.5 0.7 constant_dynamic-update-slice_fusion.1
  6.2 0.7 constant_dynamic-update-slice_fusion
  6.9 0.6 reshape.36.vectors
  7.6 158.6 %layer.1 = (bf16[2,320,768]{2,1,0:T(8,128)(2,1)}, bf16[2,320,768]{2,1,0:T(8,128)(2,1)}, f32[48,2304]{1,0:T(8,128)}, f32[48,768]{1,0:T(8,128)}, f32[48,3072]{1,0:...) custom-call(bf16[2,320,768]{2,1,0:T(8,128)(2,1)} %tokens.1, ...), custom_call_target="tpu_custom_call" | custom-call | tf_op jit(solution)/shard_map/layer/pallas_call | solution.py:647
  166.2 0.0 copy-start.2
  166.2 0.0 copy-start.1
  166.2 0.0 copy-start
  166.2 0.9 constant_dynamic-slice_fusion
  167.1 0.5 slice_bitcast_fusion
  167.6 0.7 slice.32
  168.4 0.6 dynamic_slice.7
  169.0 2.2 %copy.49 = bf16[2,320,768]{2,1,0:T(8,128)(2,1)} copy(bf16[2,320,768]{2,1,0:T(8,128)(2,1)} %get-tuple-element.52) | data formatting | bytes 1966080
  171.2 2.2 %copy.50 = bf16[2,320,768]{2,1,0:T(8,128)(2,1)} copy(bf16[2,320,768]{2,1,0:T(8,128)(2,1)} %get-tuple-element.53) | data formatting | bytes 1966080
  173.5 1.8 %copy.51 = f32[48,2304]{1,0:T(8,128)} copy(f32[48,2304]{1,0:T(8,128)} %get-tuple-element.54) | data formatting | bytes 884736
  175.3 0.0 copy-done.2
  175.3 0.7 copy.52
  175.9 0.0 copy-done.1
  175.9 0.8 copy.53
  176.7 0.0 copy-done
  176.7 0.8 copy.54
  (4 shorter events, 0.0 us)
Async XLA Ops:
  166.2 9.1 %copy-start.2 = (f32[48,768]{1,0:T(8,128)S(1)}, f32[48,768]{1,0:T(8,128)}, u32[]{:S(2)}) copy-start(f32[48,768]{1,0:T(8,128)} %get-tuple-element.57) | copy-start | bytes 442372
  166.2 9.7 %copy-start.1 = (f32[48,3072]{1,0:T(8,128)S(1)}, f32[48,3072]{1,0:T(8,128)}, u32[]{:S(2)}) copy-start(f32[48,3072]{1,0:T(8,128)} %get-tuple-element.61) | copy-start | bytes 1769476
  166.2 10.5 %copy-start = (f32[192,768]{1,0:T(8,128)S(1)}, f32[192,768]{1,0:T(8,128)}, u32[]{:S(2)}) copy-start(f32[192,768]{1,0:T(8,128)} %get-tuple-element.63) | copy-start | bytes 1769476

commit v2 on v1

--- a/solution.py
+++ b/solution.py
@@ -226,7 +226,20 @@
 UNIT_ROWS = 48
 UNITS = 12
 WEIGHT = {"c": 1, "y": 2, "l": 4, "h": 8}
-ORDERS = ("cyxlhg", "clyhxg")
+ORDERS = (
+    "clhxyg",
+    "cyxlhg",
+    "cylxhg",
+    "clyxhg",
+    "cxlyhg",
+    "cxylhg",
+    "cxylhg",
+    "cylhxg",
+    "cxlyhg",
+    "cylhxg",
+    "cxylhg",
+    "cylxhg",
+)
 SMALL_ORDER = "cylhx"
 SWAP = 0
 
@@ -261,7 +274,7 @@
             place.append(rest % size)
             rest = rest // size
         place = tuple(reversed(place)) + (slice(None), slice(None))
-        target[place] = (target[place].astype(F32) + other[place].astype(F32)).astype(BF)
+        target[place] = target[place] + other[place]
         return carry
 
     if total == 1:
@@ -327,13 +340,15 @@
 
 
 def layer_kernel(
-    tokens, cotangent, seg_align, seg_count, vectors, w_qkv, w_out, w_inner, w_outer,
-    block_output, tokens_grad, g_qkv, g_out, g_inner, g_outer, sums_out, probs_hbm,
-    x, qkv, context_t, w_out_v, normal, root, cot, acc, grad_att, sums, own, small, small_got, *rest,
+    tokens, cotangent, seg_align, seg_count,
+    query_bias, value_bias, output_bias, first_gain, first_shift, outer_bias, second_gain, second_shift, inner_bias,
+    w_qkv, w_out, w_inner, w_outer,
+    block_output, tokens_grad, shards, sums_out, probs_hbm,
+    vectors, x, qkv, context_t, w_out_v, normal, root, cot, acc, grad_att, sums, own, small, small_got, *rest,
 ):
     rest = list(rest)
-    buffers = [[rest.pop(0) for _ in ORDERS[0]] for _ in range(UNITS)]
-    unit_send, unit_recv, outer_send, outer_recv, local_sem, pair_sem, swap_send, swap_recv, small_send, small_recv = rest
+    buffers = [[rest.pop(0) for _ in ORDERS[0][:-1]] for _ in range(UNITS)]
+    unit_send, unit_recv, outer_send, outer_recv, local_sem, pair_sem, swap_send, swap_recv, small_send, small_recv, vector_sem, shard_sem = rest
     slots, features = x.shape
     half = slots // 2
     wide = w_inner.shape[1]
@@ -365,11 +380,23 @@
     keep_grad = local(x.at[mine], tokens_grad.at[seq], 4)
     swap_grad = swap(x.at[other], tokens_grad.at[seq], 3)
     keep_tokens.start()
+    rows_of = {0: query_bias, 2: value_bias, 3: output_bias, 4: first_gain, 5: first_shift, 6: outer_bias, 7: second_gain, 8: second_shift}
+    load_vectors = [pltpu.make_async_copy(ref, vectors.at[i], vector_sem.at[i]) for i, ref in rows_of.items()]
+    load_vectors += [
+        pltpu.make_async_copy(inner_bias.at[pl.ds(i * features, features)], vectors.at[9 + i], vector_sem.at[9 + i])
+        for i in range(wide // features)
+    ]
+    for copy in load_vectors:
+        copy.start()
+    vectors[1:2] = jnp.zeros((1, features), F32)
 
     units = [
-        Unit(n, own.at[n if n < 8 else n - 8], ORDERS[n % 2], buffers[n], unit_send, unit_recv, me, seq)
+        Unit(n, own.at[n if n < 8 else n - 8], ORDERS[n], buffers[n] + [shards.at[n, seq]], unit_send, unit_recv, me, seq)
         for n in range(UNITS)
     ]
+
+    def keep_shard(number):
+        return pltpu.make_async_copy(buffers[number][-1], shards.at[number, seq], shard_sem.at[number])
 
     def outer_copy(j, sub):
         hi, lo = j // 2, j % 2
@@ -396,6 +423,8 @@
             units[number].add(0)
         else:
             units[number].advance(stage)
+        if number < UNITS and stage == 4:
+            keep_shard(number).start()
 
     plan = with_stages(SCHEDULE)
 
@@ -419,6 +448,8 @@
             load_out.start()
             fill_reward(reward, seg_align[pl.ds(seq, 1), :], seg_count[seq])
             keep_tokens.wait()
+            for copy in load_vectors:
+                copy.wait()
             load_qkv.wait()
 
             def project(rows):
@@ -468,7 +499,7 @@
             load_out.wait()
             for here in columns:
                 acc[:, here] = dot(low[...], w_out_v[:, here])
-            first_norm(x, acc, b_out, gain1, shift1, normal, root, low, 32)
+            first_norm(x, acc, b_out, gain1, shift1, normal, root, low, 160)
             load_inner.wait()
 
             def inner_body(index):
@@ -484,7 +515,7 @@
                 acc[:, here] = dot(hidden[...], w_outer_v[:, here])
             keep_cot.wait()
             swap_cot.wait()
-            second_norm(normal, gain1, shift1, acc, b_outer, gain2, shift2, cot, cot, grad_second, grad_att, sums, 32)
+            second_norm(normal, gain1, shift1, acc, b_outer, gain2, shift2, cot, cot, grad_second, grad_att, sums, 160)
             keep_output.start()
             swap_output.start()
             turned_low[...] = jnp.transpose(low[...])
@@ -517,7 +548,7 @@
             for c, here in enumerate(columns):
                 acc[:, here] = dot_nt(hidden[...], w_inner_v[here, :])
                 point(("a", c))
-            first_norm_back(grad_second, acc, normal, root, gain1, acc, grad_att, sums, 32)
+            first_norm_back(grad_second, acc, normal, root, gain1, acc, grad_att, sums, 160)
 
         pl.run_scoped(
             mlp,
@@ -604,29 +635,70 @@
     swap_output.wait()
     keep_grad.wait()
     swap_grad.wait()
+    for number in range(UNITS):
+        keep_shard(number).wait()
     sums_out[...] = small[...]
+
+
+def finish_kernel(
+    block_in, grad_in, shards, sums,
+    block_output, tokens_grad, g_qkv, g_query, g_value, g_out, g_out_bias, g_gain1, g_shift1, g_inner, g_inner_bias,
+    g_outer, g_outer_bias, g_gain2, g_shift2, sem,
+):
+    copies = [
+        pltpu.make_async_copy(block_in, block_output, sem.at[0]),
+        pltpu.make_async_copy(grad_in, tokens_grad, sem.at[1]),
+    ]
+    for copy in copies:
+        copy.start()
+    me = lax.axis_index("dp")
+    features = sums.shape[1]
     size = features // 2
     for number in range(UNITS):
-        kept, got = (buffers[number][stage] for stage in (4, 5))
-        for side in range(2):
-
-            @pl.when(seq == side)
-            def _():
-                for block, place in ((kept, side), (got, 1 - side)):
-                    value = block[...].astype(F32)
-                    start = place * size
-                    if number < 4:
-                        g_outer[number * UNIT_ROWS : (number + 1) * UNIT_ROWS, start : start + size] = value
-                    elif number < 8:
-                        start += (number - 4) * features
-                        g_inner[:, start : start + size] = value
-                    elif number == 8:
-                        g_out[:, start : start + size] = value
-                    else:
-                        for piece in range(size // PAIR):
-                            column = start + piece * PAIR
-                            target = column // WIDE * features + (number - 9) * WIDE + column % WIDE
-                            g_qkv[:, target : target + PAIR] = value[:, piece * PAIR : (piece + 1) * PAIR]
+        for place in range(2):
+            value = shards[number, place].astype(F32)
+            start = place * size
+            if number < 4:
+                g_outer[number * UNIT_ROWS : (number + 1) * UNIT_ROWS, start : start + size] = value
+            elif number < 8:
+                start += (number - 4) * features
+                g_inner[:, start : start + size] = value
+            elif number == 8:
+                g_out[:, start : start + size] = value
+            else:
+                for piece in range(size // PAIR):
+                    column = start + piece * PAIR
+                    target = column // WIDE * features + (number - 9) * WIDE + column % WIDE
+                    g_qkv[:, target : target + PAIR] = value[:, piece * PAIR : (piece + 1) * PAIR]
+    rows = pltpu.roll(sums[0:8], (features - me * UNIT_ROWS) % features, 1)
+    for index, out in enumerate((g_gain2, g_shift2, g_outer_bias, g_gain1, g_shift1, g_out_bias, g_query, g_value)):
+        out[...] = rows[index, :UNIT_ROWS]
+    share = 4 * UNIT_ROWS
+    place = me * share
+    line = pltpu.roll(sums[pl.ds(8 + place // features, 1)], (features - place % features) % features, 1)
+    g_inner_bias[...] = line[0, :share]
+    for copy in copies:
+        copy.wait()
+
+
+def finish(block, grad, shards, sums, wide):
+    features = block.shape[-1]
+    S = jax.ShapeDtypeStruct
+    vector = S((UNIT_ROWS,), F32)
+    hbm, vmem = pl.BlockSpec(memory_space=pltpu.HBM), pl.BlockSpec(memory_space=pltpu.VMEM)
+    return pl.pallas_call(
+        finish_kernel,
+        name="finish",
+        out_shape=[
+            S(block.shape, BF), S(grad.shape, BF), S((UNIT_ROWS, 3 * features), F32), vector, vector,
+            S((UNIT_ROWS, features), F32), vector, vector, vector, S((UNIT_ROWS, wide), F32), S((4 * UNIT_ROWS,), F32),
+            S((4 * UNIT_ROWS, features), F32), vector, vector, vector,
+        ],
+        in_specs=[hbm, hbm, vmem, vmem],
+        out_specs=[hbm, hbm] + [vmem] * 13,
+        scratch_shapes=[pltpu.SemaphoreType.DMA((2,))],
+        compiler_params=pltpu.CompilerParams(vmem_limit_bytes=32 * 2**20),
+    )(block, grad, shards, sums)
 
 
 def layer(tokens, cotangent, seg_align, seg_count, vectors, w_qkv, w_out, w_inner, w_outer):
@@ -635,60 +707,53 @@
     pairs = features // PAIR
     S, V, D = jax.ShapeDtypeStruct, pltpu.VMEM, pltpu.SemaphoreType.DMA
     scratch = [
-        V((slots, features), BF), V((slots, 3 * features), BF), V((features, slots), BF), V(w_out.shape, BF),
+        V((16, features), F32), V((slots, features), BF), V((slots, 3 * features), BF), V((features, slots), BF), V(w_out.shape, BF),
         V((slots, features), F32), V((slots, PAIR), F32), V((slots, features), BF), V((slots, features), F32),
         V((slots, features), BF), V((16, 8, features), F32), V((8, 2, 2, 2, 2, UNIT_ROWS, features), BF),
         V((16, features), F32), V((len(SMALL_ORDER), 16, features), F32),
     ]
     for number in range(UNITS):
-        scratch += [V(shape, BF) for shape in stage_shapes(ORDERS[number % 2], UNIT_ROWS, features)]
-    scratch += [D((UNITS, 6)), D((UNITS, 6)), D((4, 4)), D((4, 4)), D((9,)), D((2,)), D((4,)), D((4,)), D((5,)), D((5,))]
+        scratch += [V(shape, BF) for shape in stage_shapes(ORDERS[number], UNIT_ROWS, features)[:-1]]
+    scratch += [D((UNITS, 6)), D((UNITS, 6)), D((4, 4)), D((4, 4)), D((9,)), D((2,)), D((4,)), D((4,)), D((5,)), D((5,)), D((16,)), D((UNITS,))]
     hbm, vmem = pl.BlockSpec(memory_space=pltpu.HBM), pl.BlockSpec(memory_space=pltpu.VMEM)
     return pl.pallas_call(
         layer_kernel,
         name="layer",
         out_shape=[
-            S(tokens.shape, BF), S(tokens.shape, BF), S((UNIT_ROWS, 3 * features), F32), S((UNIT_ROWS, features), F32),
-            S((UNIT_ROWS, wide), F32), S((4 * UNIT_ROWS, features), F32), S((16, features), F32),
+            S(tokens.shape, BF), S(tokens.shape, BF), S((UNITS, 2, UNIT_ROWS, features // 2), BF), S((16, features), F32),
             S((pairs, slots, 2 * slots), BF),
         ],
-        in_specs=[hbm, hbm, vmem, pl.BlockSpec(memory_space=pltpu.SMEM), vmem, hbm, hbm, hbm, hbm],
-        out_specs=[hbm, hbm, vmem, vmem, vmem, vmem, vmem, hbm],
+        in_specs=[hbm, hbm, vmem, pl.BlockSpec(memory_space=pltpu.SMEM)] + [hbm] * 13,
+        out_specs=[hbm, hbm, hbm, vmem, hbm],
         scratch_shapes=scratch,
         compiler_params=pltpu.CompilerParams(collective_id=0, has_side_effects=True, vmem_limit_bytes=60 * 2**20),
-    )(tokens, cotangent, seg_align, seg_count, vectors, w_qkv, w_out, w_inner, w_outer)
+    )(tokens, cotangent, seg_align, seg_count, *vectors, w_qkv, w_out, w_inner, w_outer)
 
 
 SCHEDULE = (
-    (("i", 1), (0,)),
-    (("g", 2), (1,)),
-    (("i", 2), (2,)),
-    (("g", 3), (3,)),
-    (("i", 3), (4,)),
-    (("a", 0), (5,)),
-    (("a", 1), (0, 6)),
-    (("a", 2), (1, 7)),
-    (("n", 0), (2,)),
-    (("o", 0), (0,)),
-    (("o", 1), (3,)),
-    (("v", 0), (8, 4, 2)),
-    (("r", 0), (5,)),
-    (("s", 1), (6, 4)),
-    (("u", 2), (7,)),
-    (("v", 2), (1, 0)),
-    (("r", 2), (2,)),
-    (("u", 3), (9, 3, 4, 6)),
-    (("s", 3), (1,)),
-    (("u", 4), (0, 8)),
-    (("v", 4), (2,)),
-    (("r", 4), (1,)),
-    (("u", 5), (10, 5, 0)),
-    (("r", 5), (9, 7, 8)),
-    (("s", 5), (2, 1)),
-    (("t", 0), (3,)),
-    (("t", 2), (4,)),
-    (("t", 4), (6,)),
-    (("end", 0), (11, 12, 3, 10, 4, 5, 9, 12, 7, 8, 6, 11, 3, 12, 9, 10, 8, 5, 11, 7, 12, 6, 9, 10, 8, 5, 7, 12, 11, 9, 10, 11, 10, 11)),
+    (("i", 2), (0, 1, 2, 3, 4)),
+    (("i", 3), (5,)),
+    (("a", 0), (6,)),
+    (("a", 1), (7,)),
+    (("n", 0), (0, 1)),
+    (("o", 0), (4,)),
+    (("u", 0), (8,)),
+    (("v", 0), (3, 2)),
+    (("u", 1), (5,)),
+    (("v", 2), (0, 4, 7)),
+    (("r", 2), (6,)),
+    (("u", 3), (9, 2)),
+    (("v", 3), (3, 1)),
+    (("u", 4), (7, 5)),
+    (("v", 4), (4, 1)),
+    (("u", 5), (10,)),
+    (("v", 5), (8, 6)),
+    (("s", 5), (0, 5, 7)),
+    (("t", 0), (2, 4)),
+    (("t", 2), (3,)),
+    (("t", 3), (1,)),
+    (("t", 4), (11, 12)),
+    (("end", 0), (9, 8, 0, 6, 5, 10, 7, 2, 4, 3, 11, 12, 9, 8, 6, 11, 10, 12, 1, 9, 0, 5, 8, 7, 10, 2, 3, 6, 12, 11, 10, 9, 8, 12, 11, 10, 9, 11)),
 )
 
 
@@ -944,44 +1009,13 @@
         return plain(
             tokens, seg_count, seg_align, cotangent, qkv_weight, query_bias, value_bias, output_weight, output_bias, first_gain, first_shift, inner_weight, inner_bias, outer_weight, outer_bias, second_gain, second_shift
         )
-    vectors = jnp.concatenate(
-        [
-            query_bias,
-            jnp.zeros_like(query_bias),
-            value_bias,
-            output_bias,
-            first_gain,
-            first_shift,
-            outer_bias,
-            second_gain,
-            second_shift,
-            inner_bias,
-            jnp.zeros((3 * features,), F32),
-        ]
-    ).reshape(16, features)
-    block_output, tokens_grad, g_qkv, g_out, g_inner, g_outer, sums, _ = layer(
+    vectors = (
+        query_bias, value_bias, output_bias, first_gain, first_shift, outer_bias, second_gain, second_shift, inner_bias
+    )
+    block, grad, shards, sums, _ = layer(
         tokens, cotangent, seg_align, seg_count, vectors, qkv_weight, output_weight, inner_weight, outer_weight
     )
-    place = lax.axis_index("dp")
-    rows = lax.dynamic_slice(sums, (0, place * UNIT_ROWS), (8, UNIT_ROWS))
-    inner_bias_grad = lax.dynamic_slice(sums[8:12].reshape(-1), (place * 4 * UNIT_ROWS,), (4 * UNIT_ROWS,))
-    return (
-        block_output,
-        tokens_grad,
-        g_qkv,
-        rows[6],
-        rows[7],
-        g_out,
-        rows[5],
-        rows[3],
-        rows[4],
-        g_inner,
-        inner_bias_grad,
-        g_outer,
-        rows[2],
-        rows[0],
-        rows[1],
-    )
+    return tuple(finish(block, grad, shards, sums, inner_weight.shape[1]))
 
 
 def solution(mesh):

time: 178 us -> 153 us (0.86)
  local copies, waits for them, and re-layouts: 18.2 us -> 4.36 us
  Pallas kernels: 159 us -> 148 us
    pallas_call x1, Pallas kernels: 159 us -> 145 us  [layer(): pl.pallas_call(layer_kernel, name='layer', out_shape=[S(tokens.shape, BF)...]
    unnamed x22 -> x8, local copies, waits for them, and re-layouts: 14.8 us -> 4.36 us
    pallas_call x0 -> x1, Pallas kernels: none -> 2.52 us  [finish(): pl.pallas_call(finish_kernel, name='finish', out_shape=[S(block.shape, BF...]
where the time goes in v2:
time: 153 us
  Pallas kernels  148 us (97%)
  local copies, waits for them, and re-layouts  4.36 us (3%)
    pallas_call x1, Pallas kernels, layer(): pl.pallas_call(layer_kernel, name='layer', out_shape=[S(tokens.shape, BF)...  145 us
    unnamed x8, local copies, waits for them, and re-layouts  4.36 us

profile of v2, /device:TPU:0, one launch (start us, length us, event | category | flops | bytes accessed | tf_op | source)
XLA Modules:
  0.0 152.7 jit_solution(12410290411326965113)
XLA Ops:
  0.7 145.0 %layer.1 = (bf16[2,320,768]{2,1,0:T(8,128)(2,1)}, bf16[2,320,768]{2,1,0:T(8,128)(2,1)}, bf16[12,2,48,384]{3,2,1,0:T(8,128)(2,1)}, f32[16,768]{1,0:T(8,128)}, bf16[6,640,1280]{2,1,0:T(8,128)(2,1)}) custom-call(bf16[2,320,768]{2,1,0:T(8,128)(2,1)} %tokens.1, bf16[2,320,768]{2,1,0:T(8,128)(2,1)} %cotangent.1, s32[2,512]{1,0:T(2,128)} %seg_align.1, s32[2]{0:T(128)} %seg_count.1, ...), custom_call_target="tpu_custom_call" | custom-call | tf_op jit(solution)/shard_map/layer/pallas_call | solution.py:719
  145.7 0.0 copy-start
  145.7 1.2 copy-done
  146.9 0.0 copy-start.1
  146.9 1.2 copy-done.1
  148.1 0.0 copy-start.2
  148.1 1.2 copy-done.2
  149.2 0.0 copy-start.3
  149.2 0.8 copy-done.3
  150.0 2.5 %finish.1 = (bf16[2,320,768]{2,1,0:T(8,128)(2,1)}, bf16[2,320,768]{2,1,0:T(8,128)(2,1)}, f32[48,2304]{1,0:T(8,128)}, f32[48]{0:T(128)}, f32[48]{0:T(128)}, /*ind...) custom-call(bf16[2,320,768]{2,1,0:T(8,128)(2,1)S(1)} %copy-done, ...), custom_call_target="tpu_custom_call" | custom-call | tf_op jit(solution)/shard_map/finish/pallas_call | solution.py:689
Async XLA Ops:
  145.7 1.2 copy-start
  146.9 1.2 copy-start.1
  148.1 1.2 copy-start.2
  149.2 0.8 copy-start.3

commit v3 on v2

--- a/solution.py
+++ b/solution.py
@@ -98,9 +98,8 @@
             block = slice(chunk * WIDE, (chunk + 1) * WIDE)
             scores = dot_nt(keys, both[block, :]) * scaling + reward[:, block]
             scores = jnp.exp2(scores - jnp.max(scores, axis=0, keepdims=True))
-            low = (scores * (1.0 / jnp.sum(scores, axis=0, keepdims=True))).astype(BF)
-            probs[:, block] = low
-            side[:, block] = dot(turned[...], low).astype(BF)
+            probs[:, block] = (scores * (1.0 / jnp.sum(scores, axis=0, keepdims=True))).astype(BF)
+        side[...] = dot(turned[...], probs[...]).astype(BF)
         context_t[at(pair * PAIR, HEAD), :] = side[:HEAD, :slots]
         context_t[at(pair * PAIR + HEAD, HEAD), :] = side[HEAD:, slots:]
 
@@ -209,10 +208,10 @@
             mean = jnp.sum(weight * pull, axis=0, keepdims=True)
             low = (weight * (pull - mean)).astype(BF)
             scores[:, block] = low
-            side[:, block] = dot(turned[...], low)
             if chunk == 2:
                 points("u", pair)
         points("v", pair)
+        side[...] = dot(turned[...], scores[...])
         grad_qkv[:, there] = (dot(scores[...], both[...]) * scaling).astype(BF)
         grad_qkv[:, last] = dot(probs[...], both_grad[...]).astype(BF)
         mine = jnp.concatenate([side[:HEAD, :slots], side[HEAD:, slots:]], axis=0)
@@ -518,6 +517,7 @@
             second_norm(normal, gain1, shift1, acc, b_outer, gain2, shift2, cot, cot, grad_second, grad_att, sums, 160)
             keep_output.start()
             swap_output.start()
+
             turned_low[...] = jnp.transpose(low[...])
 
             def outer_step(j):
@@ -643,14 +643,19 @@
 def finish_kernel(
     block_in, grad_in, shards, sums,
     block_output, tokens_grad, g_qkv, g_query, g_value, g_out, g_out_bias, g_gain1, g_shift1, g_inner, g_inner_bias,
-    g_outer, g_outer_bias, g_gain2, g_shift2, sem,
+    g_outer, g_outer_bias, g_gain2, g_shift2, passed, sem,
 ):
-    copies = [
-        pltpu.make_async_copy(block_in, block_output, sem.at[0]),
-        pltpu.make_async_copy(grad_in, tokens_grad, sem.at[1]),
-    ]
-    for copy in copies:
+    ins, outs = [], []
+    for index, (source, target) in enumerate(((block_in, block_output), (grad_in, tokens_grad))):
+        for part in range(2):
+            buffer, number = passed.at[index, part], 2 * index + part
+            ins.append(pltpu.make_async_copy(source.at[part], buffer, sem.at[0, number]))
+            outs.append(pltpu.make_async_copy(buffer, target.at[part], sem.at[1, number]))
+    for copy in ins:
         copy.start()
+    for copy, onward in zip(ins, outs):
+        copy.wait()
+        onward.start()
     me = lax.axis_index("dp")
     features = sums.shape[1]
     size = features // 2
@@ -677,7 +682,7 @@
     place = me * share
     line = pltpu.roll(sums[pl.ds(8 + place // features, 1)], (features - place % features) % features, 1)
     g_inner_bias[...] = line[0, :share]
-    for copy in copies:
+    for copy in outs:
         copy.wait()
 
 
@@ -696,8 +701,8 @@
         ],
         in_specs=[hbm, hbm, vmem, vmem],
         out_specs=[hbm, hbm] + [vmem] * 13,
-        scratch_shapes=[pltpu.SemaphoreType.DMA((2,))],
-        compiler_params=pltpu.CompilerParams(vmem_limit_bytes=32 * 2**20),
+        scratch_shapes=[pltpu.VMEM((2,) + block.shape, BF), pltpu.SemaphoreType.DMA((2, 4))],
+        compiler_params=pltpu.CompilerParams(vmem_limit_bytes=60 * 2**20),
     )(block, grad, shards, sums)
 
 

time: 153 us -> 135 us (0.88)
  Pallas kernels: 148 us -> 134 us
  local copies, waits for them, and re-layouts: 4.36 us -> 0 us
    pallas_call x1, Pallas kernels: 145 us -> 129 us  [layer(): pl.pallas_call(layer_kernel, name='layer', out_shape=[S(tokens.shape, BF)...]
    unnamed x8 -> x0, local copies, waits for them, and re-layouts: 4.36 us -> none
    pallas_call x1, Pallas kernels: 2.52 us -> 4.79 us  [finish(): pl.pallas_call(finish_kernel, name='finish', out_shape=[S(block.shape, BF...]
where the time goes in v3:
time: 135 us
  Pallas kernels  134 us (99%)
    pallas_call x1, Pallas kernels, layer(): pl.pallas_call(layer_kernel, name='layer', out_shape=[S(tokens.shape, BF)...  129 us
    pallas_call x1, Pallas kernels, finish(): pl.pallas_call(finish_kernel, name='finish', out_shape=[S(block.shape, BF...  4.79 us

profile of v3, /device:TPU:0, one launch (start us, length us, event | category | flops | bytes accessed | tf_op | source)
XLA Modules:
  0.0 135.0 jit_solution(11679103432728775604)
XLA Ops:
  0.7 129.4 %layer.1 = (bf16[2,320,768]{2,1,0:T(8,128)(2,1)}, bf16[2,320,768]{2,1,0:T(8,128)(2,1)}, bf16[12,2,48,384]{3,2,1,0:T(8,128)(2,1)}, f32[16,768]{1,0:T(8,128)}, bf16[6,640,1280]{2,1,0:T(8,128)(2,1)}) custom-call(bf16[2,320,768]{2,1,0:T(8,128)(2,1)} %tokens.1, bf16[2,320,768]{2,1,0:T(8,128)(2,1)} %cotangent.1, s32[2,512]{1,0:T(2,128)} %seg_align.1, s32[2]{0:T(128)} %seg_count.1, ...), custom_call_target="tpu_custom_call" | custom-call | tf_op jit(solution)/shard_map/layer/pallas_call | solution.py:724
  130.1 4.8 %finish.1 = (bf16[2,320,768]{2,1,0:T(8,128)(2,1)}, bf16[2,320,768]{2,1,0:T(8,128)(2,1)}, f32[48,2304]{1,0:T(8,128)}, f32[48]{0:T(128)}, f32[48]{0:T(128)}, /*ind...) custom-call(bf16[2,320,768]{2,1,0:T(8,128)(2,1)} %get-tuple-element., ...), custom_call_target="tpu_custom_call" | custom-call | tf_op jit(solution)/shard_map/finish/pallas_call | solution.py:694

commit v4 on v3

--- a/solution.py
+++ b/solution.py
@@ -226,17 +226,17 @@
 UNITS = 12
 WEIGHT = {"c": 1, "y": 2, "l": 4, "h": 8}
 ORDERS = (
-    "clhxyg",
-    "cyxlhg",
+    "cylhxg",
     "cylxhg",
-    "clyxhg",
-    "cxlyhg",
     "cxylhg",
     "cxylhg",
-    "cylhxg",
-    "cxlyhg",
-    "cylhxg",
-    "cxylhg",
+    "clxhyg",
+    "cyxlhg",
+    "cyxlhg",
+    "clyhxg",
+    "cylxhg",
+    "cxlhyg",
+    "cylxhg",
     "cylxhg",
 )
 SMALL_ORDER = "cylhx"
@@ -328,7 +328,7 @@
 
 
 def with_stages(schedule):
-    reached = [0] * (UNITS + 1)
+    reached = [1] * 4 + [0] * (UNITS - 3)
     plan = {}
     for point, numbers in schedule:
         steps = plan.setdefault(point, [])
@@ -347,7 +347,7 @@
 ):
     rest = list(rest)
     buffers = [[rest.pop(0) for _ in ORDERS[0][:-1]] for _ in range(UNITS)]
-    unit_send, unit_recv, outer_send, outer_recv, local_sem, pair_sem, swap_send, swap_recv, small_send, small_recv, vector_sem, shard_sem = rest
+    unit_send, unit_recv, outer_send, outer_recv, local_sem, pair_sem, swap_send, swap_recv, small_send, small_recv, vector_sem, shard_sem, chunk_send, chunk_recv = rest
     slots, features = x.shape
     half = slots // 2
     wide = w_inner.shape[1]
@@ -405,6 +405,25 @@
             send_sem=outer_send.at[j, sub], recv_sem=outer_recv.at[j, sub],
             device_id=partner_of("c", me, seq), device_id_type=MESH)
 
+    def chunk_copy(j, sub):
+        bit, held = ORDERS[sub][1], buffers[sub][0].at[j // 2, j % 2]
+        if bit == "x":
+            size = features // 2
+            given = held.at[:, :, pl.ds(pl.multiple_of((1 - seq) * size, PAIR), size)]
+        else:
+            given = held.at[1 - (me // WEIGHT[bit]) % 2]
+        return pltpu.make_async_remote_copy(
+            src_ref=given,
+            dst_ref=buffers[sub][1].at[j // 2, j % 2],
+            send_sem=chunk_send.at[j, sub], recv_sem=chunk_recv.at[j, sub],
+            device_id=partner_of(bit, me, seq), device_id_type=MESH)
+
+    def take_chunk(j):
+        for sub in range(4):
+            outer_copy(j, sub).wait()
+            add_into(buffers[sub][0].at[j // 2, j % 2], own.at[sub, j // 2, j % 2, :, core])
+            chunk_copy(j, sub).start()
+
     def small_copy(stage):
         return pltpu.make_async_remote_copy(
             src_ref=small, dst_ref=small_got.at[stage], send_sem=small_send.at[stage], recv_sem=small_recv.at[stage],
@@ -416,10 +435,10 @@
             small[...] += small_got[stage]
             if stage + 1 < len(SMALL_ORDER):
                 small_copy(stage + 1).start()
-        elif number < 4 and stage == 0:
+        elif number < 4 and stage == 1:
             for j in range(4):
-                outer_copy(j, number).wait()
-            units[number].add(0)
+                chunk_copy(j, number).wait()
+            units[number].add(1)
         else:
             units[number].advance(stage)
         if number < UNITS and stage == 4:
@@ -453,11 +472,11 @@
 
             def project(rows):
                 def body(index):
-                    here = at(index * WIDE, WIDE)
-                    bias = vectors[pl.ds(index // 3, 1), at(index % 3 * WIDE, WIDE)]
+                    here = at(index * features, features)
+                    bias = vectors[pl.ds(index, 1), :]
                     qkv[rows, here] = (dot(x[rows, :], w_qkv_v[:, here]) + bias).astype(BF)
 
-                loop(3 * features // WIDE, body)
+                loop(3, body)
 
             project(mine)
             load_inner.start()
@@ -502,13 +521,13 @@
             load_inner.wait()
 
             def inner_body(index):
-                here = at(index * WIDE, WIDE)
-                bias = vectors[pl.ds(9 + index // 3, 1), at(index % 3 * WIDE, WIDE)]
+                here = at(index * features, features)
+                bias = vectors[pl.ds(9 + index, 1), :]
                 value, grade = gate(dot(low[...], w_inner_v[:, here]) + bias)
                 hidden[:, here] = value.astype(BF)
                 slope[:, here] = grade.astype(BF)
 
-            loop(wide // WIDE, inner_body)
+            loop(wide // features, inner_body)
             load_outer.wait()
             for here in columns:
                 acc[:, here] = dot(hidden[...], w_outer_v[:, here])
@@ -516,9 +535,7 @@
             swap_cot.wait()
             second_norm(normal, gain1, shift1, acc, b_outer, gain2, shift2, cot, cot, grad_second, grad_att, sums, 160)
             keep_output.start()
-            swap_output.start()
-
-            turned_low[...] = jnp.transpose(low[...])
+
 
             def outer_step(j):
                 block = dot_tn(hidden[:, at(j * features, features)], grad_att[...]).astype(BF)
@@ -527,8 +544,12 @@
                     own[sub, j // 2, j % 2] = block[:, :, sub]
                 for sub in range(4):
                     outer_copy(j, sub).start()
+                pl.when(j >= 2)(lambda: take_chunk(j - 2))
 
             loop(4, outer_step)
+            take_chunk(2)
+            turned_low[...] = jnp.transpose(low[...])
+            take_chunk(3)
 
             def inner_step(j):
                 here = at(j * features, features)
@@ -545,6 +566,7 @@
                 points("i", j, 4)
 
             loop(4, inner_step)
+            swap_output.start()
             for c, here in enumerate(columns):
                 acc[:, here] = dot_nt(hidden[...], w_inner_v[here, :])
                 point(("a", c))
@@ -719,7 +741,7 @@
     ]
     for number in range(UNITS):
         scratch += [V(shape, BF) for shape in stage_shapes(ORDERS[number], UNIT_ROWS, features)[:-1]]
-    scratch += [D((UNITS, 6)), D((UNITS, 6)), D((4, 4)), D((4, 4)), D((9,)), D((2,)), D((4,)), D((4,)), D((5,)), D((5,)), D((16,)), D((UNITS,))]
+    scratch += [D((UNITS, 6)), D((UNITS, 6)), D((4, 4)), D((4, 4)), D((9,)), D((2,)), D((4,)), D((4,)), D((5,)), D((5,)), D((16,)), D((UNITS,)), D((4, 4)), D((4, 4))]
     hbm, vmem = pl.BlockSpec(memory_space=pltpu.HBM), pl.BlockSpec(memory_space=pltpu.VMEM)
     return pl.pallas_call(
         layer_kernel,
@@ -736,29 +758,32 @@
 
 
 SCHEDULE = (
-    (("i", 2), (0, 1, 2, 3, 4)),
+    (("i", 2), (4,)),
     (("i", 3), (5,)),
-    (("a", 0), (6,)),
+    (("a", 0), (0, 2, 6, 1, 3)),
     (("a", 1), (7,)),
-    (("n", 0), (0, 1)),
-    (("o", 0), (4,)),
+    (("n", 0), (4,)),
+    (("o", 1), (5, 0)),
     (("u", 0), (8,)),
-    (("v", 0), (3, 2)),
-    (("u", 1), (5,)),
-    (("v", 2), (0, 4, 7)),
-    (("r", 2), (6,)),
-    (("u", 3), (9, 2)),
-    (("v", 3), (3, 1)),
-    (("u", 4), (7, 5)),
-    (("v", 4), (4, 1)),
-    (("u", 5), (10,)),
-    (("v", 5), (8, 6)),
-    (("s", 5), (0, 5, 7)),
-    (("t", 0), (2, 4)),
-    (("t", 2), (3,)),
-    (("t", 3), (1,)),
-    (("t", 4), (11, 12)),
-    (("end", 0), (9, 8, 0, 6, 5, 10, 7, 2, 4, 3, 11, 12, 9, 8, 6, 11, 10, 12, 1, 9, 0, 5, 8, 7, 10, 2, 3, 6, 12, 11, 10, 9, 8, 12, 11, 10, 9, 11)),
+    (("v", 0), (2,)),
+    (("r", 0), (1,)),
+    (("s", 1), (4,)),
+    (("u", 2), (6,)),
+    (("v", 2), (7, 5)),
+    (("u", 3), (9, 1, 3)),
+    (("v", 3), (0, 2)),
+    (("s", 3), (6,)),
+    (("u", 4), (4, 5)),
+    (("r", 4), (1,)),
+    (("u", 5), (10, 8, 3)),
+    (("v", 5), (2,)),
+    (("r", 5), (6, 9)),
+    (("s", 5), (7, 0, 4, 5, 1)),
+    (("t", 0), (2,)),
+    (("t", 3), (8,)),
+    (("t", 4), (11, 0, 12)),
+    (("t", 5), (4, 3)),
+    (("end", 0), (5, 6, 10, 9, 7, 11, 10, 12, 9, 8, 3, 11, 6, 9, 12, 7, 8, 10, 11, 12, 9, 7, 10, 8, 11, 12, 10, 11)),
 )
 
 

time: 135 us -> 131 us (0.970)
  Pallas kernels: 134 us -> 130 us
    pallas_call x1, Pallas kernels: 129 us -> 125 us  [layer(): pl.pallas_call(layer_kernel, name='layer', out_shape=[S(tokens.shape, BF)...]
where the time goes in v4:
time: 131 us
  Pallas kernels  130 us (99%)
    pallas_call x1, Pallas kernels, layer(): pl.pallas_call(layer_kernel, name='layer', out_shape=[S(tokens.shape, BF)...  125 us
    pallas_call x1, Pallas kernels, finish(): pl.pallas_call(finish_kernel, name='finish', out_shape=[S(block.shape, BF...  4.79 us

profile of v4, /device:TPU:0, one launch (start us, length us, event | category | flops | bytes accessed | tf_op | source)
XLA Modules:
  0.0 130.6 jit_solution(15897552000283091163)
XLA Ops:
  0.7 125.0 %layer.1 = (bf16[2,320,768]{2,1,0:T(8,128)(2,1)}, bf16[2,320,768]{2,1,0:T(8,128)(2,1)}, bf16[12,2,48,384]{3,2,1,0:T(8,128)(2,1)}, f32[16,768]{1,0:T(8,128)}, bf16[6,640,1280]{2,1,0:T(8,128)(2,1)}) custom-call(bf16[2,320,768]{2,1,0:T(8,128)(2,1)} %tokens.1, bf16[2,320,768]{2,1,0:T(8,128)(2,1)} %cotangent.1, s32[2,512]{1,0:T(2,128)} %seg_align.1, s32[2]{0:T(128)} %seg_count.1, ...), custom_call_target="tpu_custom_call" | custom-call | tf_op jit(solution)/shard_map/layer/pallas_call | solution.py:746
  125.7 4.8 %finish.1 = (bf16[2,320,768]{2,1,0:T(8,128)(2,1)}, bf16[2,320,768]{2,1,0:T(8,128)(2,1)}, f32[48,2304]{1,0:T(8,128)}, f32[48]{0:T(128)}, f32[48]{0:T(128)}, /*ind...) custom-call(bf16[2,320,768]{2,1,0:T(8,128)(2,1)} %get-tuple-element., ...), custom_call_target="tpu_custom_call" | custom-call | tf_op jit(solution)/shard_map/finish/pallas_call | solution.py:716

commit v5 on v4

--- a/solution.py
+++ b/solution.py
@@ -517,7 +517,7 @@
             load_out.wait()
             for here in columns:
                 acc[:, here] = dot(low[...], w_out_v[:, here])
-            first_norm(x, acc, b_out, gain1, shift1, normal, root, low, 160)
+            first_norm(x, acc, b_out, gain1, shift1, normal, root, low, 320)
             load_inner.wait()
 
             def inner_body(index):
@@ -533,7 +533,7 @@
                 acc[:, here] = dot(hidden[...], w_outer_v[:, here])
             keep_cot.wait()
             swap_cot.wait()
-            second_norm(normal, gain1, shift1, acc, b_outer, gain2, shift2, cot, cot, grad_second, grad_att, sums, 160)
+            second_norm(normal, gain1, shift1, acc, b_outer, gain2, shift2, cot, cot, grad_second, grad_att, sums, 320)
             keep_output.start()
 
 
@@ -570,7 +570,7 @@
             for c, here in enumerate(columns):
                 acc[:, here] = dot_nt(hidden[...], w_inner_v[here, :])
                 point(("a", c))
-            first_norm_back(grad_second, acc, normal, root, gain1, acc, grad_att, sums, 160)
+            first_norm_back(grad_second, acc, normal, root, gain1, acc, grad_att, sums, 320)
 
         pl.run_scoped(
             mlp,

time: 131 us -> 131 us (level)
  no operation moved by 1% of the time
where the time goes in v5:
time: 131 us; the launch traced here: 130 us
  Pallas kernels  130 us (99%)
    pallas_call x1, Pallas kernels, layer(): pl.pallas_call(layer_kernel, name='layer', out_shape=[S(tokens.shape, BF)...  125 us
    pallas_call x1, Pallas kernels, finish(): pl.pallas_call(finish_kernel, name='finish', out_shape=[S(block.shape, BF...  4.79 us

profile of v5, /device:TPU:0, one launch (start us, length us, event | category | flops | bytes accessed | tf_op | source)
XLA Modules:
  0.0 130.4 jit_solution(2807812920114278877)
XLA Ops:
  0.7 124.7 %layer.1 = (bf16[2,320,768]{2,1,0:T(8,128)(2,1)}, bf16[2,320,768]{2,1,0:T(8,128)(2,1)}, bf16[12,2,48,384]{3,2,1,0:T(8,128)(2,1)}, f32[16,768]{1,0:T(8,128)}, bf16[6,640,1280]{2,1,0:T(8,128)(2,1)}) custom-call(bf16[2,320,768]{2,1,0:T(8,128)(2,1)} %tokens.1, bf16[2,320,768]{2,1,0:T(8,128)(2,1)} %cotangent.1, s32[2,512]{1,0:T(2,128)} %seg_align.1, s32[2]{0:T(128)} %seg_count.1, ...), custom_call_target="tpu_custom_call" | custom-call | tf_op jit(solution)/shard_map/layer/pallas_call | solution.py:746
  125.4 4.8 %finish.1 = (bf16[2,320,768]{2,1,0:T(8,128)(2,1)}, bf16[2,320,768]{2,1,0:T(8,128)(2,1)}, f32[48,2304]{1,0:T(8,128)}, f32[48]{0:T(128)}, f32[48]{0:T(128)}, /*ind...) custom-call(bf16[2,320,768]{2,1,0:T(8,128)(2,1)} %get-tuple-element., ...), custom_call_target="tpu_custom_call" | custom-call | tf_op jit(solution)/shard_map/finish/pallas_call | solution.py:716
